TPU v7x, 32 devices: a whole 2x2x4 slice. The times are simulated.
32 devices in a mesh: seq: 8 (over z, x), tp: 4 (over y, core).
Axes of the slice: x: 2, y: 2, z: 4, core: 2. Of those that a mesh axis runs over, the one named last changes fastest.
Arguments:
- image_in: float32 [8, 1296, 768], P('seq', 'tp'), may hold values from -6 to 6
- text_in: float32 [8, 128, 768], P('seq', 'tp'), may hold values from -6 to 6
- w_window: bfloat16 [3, 768, 768], P(None, 'seq', 'tp'), may hold values from -0.21875 to 0.21875
- w_window_out: bfloat16 [768, 768], P('tp', 'seq'), may hold values from -1.75 to 1.75
- w_text: bfloat16 [3, 768, 768], P(None, 'seq', 'tp'), may hold values from -0.21875 to 0.21875
- w_text_out: bfloat16 [768, 768], P('tp', 'seq'), may hold values from -2.5 to 2.5
- w_cross: bfloat16 [3, 768, 768], P(None, 'seq', 'tp'), may hold values from -0.21875 to 0.21875
- w_cross_out: bfloat16 [768, 768], P('tp', 'seq'), may hold values from -3.5 to 3.5
- w_up: bfloat16 [768, 3072], P('seq', 'tp'), may hold values from -0.21875 to 0.21875
- w_down: bfloat16 [3072, 768], P('tp', 'seq'), may hold values from -0.109375 to 0.109375
- gain_window: float32 [768], replicated, may hold values from 0.5 to 1.5
- gain_text: float32 [768], replicated, may hold values from 0.5 to 1.5
- gain_cross: float32 [768], replicated, may hold values from 0.5 to 1.5
- gain_memory: float32 [768], replicated, may hold values from 0.5 to 1.5
- gain_mlp: float32 [768], replicated, may hold values from 0.5 to 1.5
- page_dims: int32 [8, 2], P('seq'), may hold values from 1 to 3
- shifts: int32 [8, 2], P('seq'), may hold values from 0 to 11
- text_length: int32 [8], P('seq'), may hold values from 1 to 128
- image_cotan: float32 [8, 1296, 768], P('seq', 'tp'), may hold values from -6 to 6
- text_cotan: float32 [8, 128, 768], P('seq', 'tp'), may hold values from -6 to 6
Outputs:
- image_out: float32 [8, 1296, 768], P('seq', 'tp')
- text_out: float32 [8, 128, 768], P('seq', 'tp')
- image_grad: float32 [8, 1296, 768], P('seq', 'tp')
- text_grad: float32 [8, 128, 768], P('seq', 'tp')
- grad_window: float32 [3, 768, 768], P(None, 'seq', 'tp')
- grad_window_out: float32 [768, 768], P('tp', 'seq')
- grad_text: float32 [3, 768, 768], P(None, 'seq', 'tp')
- grad_text_out: float32 [768, 768], P('tp', 'seq')
- grad_cross: float32 [3, 768, 768], P(None, 'seq', 'tp')
- grad_cross_out: float32 [768, 768], P('tp', 'seq')
- grad_up: float32 [768, 3072], P('seq', 'tp')
- grad_down: float32 [3072, 768], P('tp', 'seq')
- grad_gain_window: float32 [768], replicated
- grad_gain_text: float32 [768], replicated
- grad_gain_cross: float32 [768], replicated
- grad_gain_memory: float32 [768], replicated
- grad_gain_mlp: float32 [768], replicated
All inputs are finite; a program needn't handle non-finite values.
Results may differ from a plain program's by a relative error of at most 0.023.
Values may be sent and summed in bfloat16 or wider, within the bound.
A program may use at most 192 MiB of HBM per device.

v0:
```python
import functools
from types import SimpleNamespace

import jax
import jax.numpy as jnp
from jax import lax
from jax.experimental import pallas as pl
from jax.experimental.pallas import tpu as pltpu
from jax.sharding import PartitionSpec as P

HD = 64
WIN = 12
GRID = 3
SIDE = GRID * WIN
AREA = WIN * WIN
COUNT = GRID * GRID
EPS = 1e-05
NEG = -1e30
SCALE = HD ** (-0.5)
F32 = jnp.float32
BF = jnp.bfloat16
MESH = pl.DeviceIdType.MESH
GELU_C = 0.7978845608028654
GELU_A = 0.044715


def nn(a, b):
    return lax.dot_general(a, b, (((1,), (0,)), ((), ())), preferred_element_type=F32)


def nt(a, b):
    return lax.dot_general(a, b, (((1,), (1,)), ((), ())), preferred_element_type=F32)


def tn(a, b):
    return lax.dot_general(a, b, (((0,), (0,)), ((), ())), preferred_element_type=F32)


def ln_fwd(v):
    center = v - jnp.mean(v, -1, keepdims=True)
    rstd = lax.rsqrt(jnp.mean(center * center, -1, keepdims=True) + EPS)
    return center * rstd, rstd


def ln_bwd(h, xh, rstd):
    return rstd * (
        h - jnp.mean(h, -1, keepdims=True) - xh * jnp.mean(h * xh, -1, keepdims=True)
    )


def head_masks(width):
    lane = lax.broadcasted_iota(jnp.int32, (1, width), 1) // HD
    return [lane == h for h in range(width // HD)]


def stack_heads(v, masks):
    return jnp.concatenate(
        [v * jnp.where(m, 1.0, 0.0).astype(BF) for m in masks], 0
    )


def merge_heads(v3, masks):
    n = v3.shape[0] // len(masks)
    out = jnp.where(masks[0], v3[:n], 0.0)
    for h in range(1, len(masks)):
        out = out + jnp.where(masks[h], v3[h * n : (h + 1) * n], 0.0)
    return out


def attend(q, k, v, allowed, masks):
    s = nt(stack_heads(q, masks), k)
    s = jnp.where(allowed, s, NEG)
    e = jnp.exp(s - jnp.max(s, -1, keepdims=True))
    p = (e * (1.0 / jnp.sum(e, -1, keepdims=True))).astype(BF)
    return merge_heads(nn(p, v), masks).astype(BF), p


def attend_back(q, k, v, p, da, masks):
    das = stack_heads(da, masks)
    dp = nt(das, v)
    pf = p.astype(F32)
    pd = pf * dp
    ds = (pd - pf * jnp.sum(pd, -1, keepdims=True)).astype(BF)
    dq = (merge_heads(nn(ds, k), masks) * SCALE).astype(BF)
    dk = tn(ds, stack_heads(q, masks)).astype(BF)
    dv = tn(p, das).astype(BF)
    return dq, dk, dv


NSEM = 192


def kernel(cfg, *refs):
    r = SimpleNamespace(**dict(zip(cfg.names, refs)))
    D, wd, hid, IR, TR, nz, sr, fused = (
        cfg.D, cfg.wd, cfg.hid, cfg.IR, cfg.TR, cfg.nz, cfg.sr, cfg.fused,
    )
    image_shard = cfg.image_shard
    IP = 4 * IR
    TP = 4 * TR
    masks = head_masks(wd)

    tp = lax.axis_index("tp")
    sq = lax.axis_index("seq")
    y, c = tp // 2, tp % 2
    core = {"tp": y * 2 + (1 - c)}
    yp = {"tp": (1 - y) * 2 + c}
    diag = {"tp": (1 - y) * 2 + (1 - c)}
    peers = (core, yp, diag)
    z, x = sq // 2, sq % 2

    def zid(d):
        return (z + d) % nz

    def zback(d):
        return (z + nz - d) % nz

    xpeer = {"seq": z * 2 + (1 - x)}

    def zpeer(d):
        return {"seq": zid(d) * 2 + x}

    cut = image_shard // 8 * 8
    whole = pl.ds(0, cut)
    rest = pl.ds(cut, image_shard - cut)

    def rows_in(i, src, buf):
        return [
            pltpu.make_async_copy(src.at[whole, 0], buf.at[whole], r.lsem.at[5 + 2 * i]),
            pltpu.make_async_copy(src.at[rest, 0], r.TL.at[i], r.lsem.at[6 + 2 * i]),
        ]

    def rows_out(i, buf, dst):
        r.TL[i] = buf[cut:image_shard]
        cps = [
            pltpu.make_async_copy(buf.at[whole], dst.at[whole, 0], r.lsem.at[5 + 2 * i]),
            pltpu.make_async_copy(r.TL.at[i], dst.at[rest, 0], r.lsem.at[6 + 2 * i]),
        ]
        for cp in cps:
            cp.start()
        return cps

    first = rows_in(0, r.image, r.MID) + rows_in(1, r.icot, r.GM)
    for cp in first:
        cp.start()

    barrier = pltpu.get_barrier_semaphore()
    greet = list(peers)
    if fused:
        greet += [xpeer] + [zpeer(d) for d in range(1, nz)]
    for dev in greet:
        pl.semaphore_signal(barrier, inc=1, device_id=dev, device_id_type=MESH)
    pl.semaphore_wait(barrier, len(greet))

    counter = [0]
    pending = []

    def push(src, dst, dev, land=None):
        k = counter[0]
        counter[0] += 1
        mk = functools.partial(
            pltpu.make_async_remote_copy,
            send_sem=r.ssem.at[k],
            recv_sem=r.rsem.at[k],
            device_id=dev,
            device_id_type=MESH,
        )
        cp = mk(src_ref=src, dst_ref=dst)
        cp.start()
        if land is not None:
            cp = mk(src_ref=src, dst_ref=land)
        pending.append(cp)
        return cp

    def sent(cps):
        for cp in cps:
            cp.wait_send()
        pending[:] = [a for a in pending if all(a is not b for b in cps)]

    def rows_of(seq_index):
        return pl.ds(pl.multiple_of(seq_index * sr, sr), sr)

    wz, wx = {}, {}

    def w_send(g):
        if not fused:
            return
        own = r.W.at[g, rows_of(sq)]
        wz[g] = [
            push(own, own, zpeer(d), r.W.at[g, rows_of(zback(d) * 2 + x)])
            for d in range(1, nz)
        ]
        wx[g] = [push(own, own, xpeer, r.W.at[g, rows_of(z * 2 + (1 - x))])]

    def w_relay(g):
        if not fused:
            return
        for d in range(1, nz):
            wz[g][d - 1].wait_recv()
            at = rows_of(zback(d) * 2 + x)
            wx[g].append(
                push(r.W.at[g, at], r.W.at[g, at], xpeer, r.W.at[g, rows_of(zback(d) * 2 + (1 - x))])
            )

    def w_ready(g):
        if not fused:
            return
        for cp in wx[g]:
            cp.wait_recv()
        sent(wz[g] + wx[g])

    def w_pack(g):
        if g < 3:
            w, out = ((r.w_window, r.w_window_out), (r.w_text, r.w_text_out), (r.w_cross, r.w_cross_out))[g]
            full = [w[j].astype(F32) for j in range(3)] + [jnp.swapaxes(out[...].astype(F32), 0, 1)]
            full = jnp.concatenate(full, 1)
        elif g == 3:
            full = r.w_up[...]
        else:
            full = r.w_down[...]
        r.W[g, rows_of(sq)] = full.astype(BF)

    if fused:
        w_pack(0)
        w_send(0)
    else:
        local = [pltpu.make_async_copy(r.wfull.at[g], r.W.at[g], r.lsem.at[g]) for g in range(5)]
        for cp in local:
            cp.start()

    size_r, size_c = r.page_dims[0, 0], r.page_dims[0, 1]
    shift_r, shift_c = r.shifts[0, 0], r.shifts[0, 1]
    length = r.text_length[0]
    lines = image_shard // SIDE

    def split_by(v, n):
        q = lax.shift_right_logical(v * ((1 << 18) // n + 1), 18)
        return q, v - q * n

    def wrap(v):
        return jnp.where(v >= SIDE, v - SIDE, v)

    def counts(row, col):
        return (split_by(row, WIN)[0] < size_r) & (split_by(col, WIN)[0] < size_c)

    def window_rows(w, a):
        ar, ac = split_by(a, WIN)
        return wrap(w // GRID * WIN + ar + shift_r), wrap(w % GRID * WIN + ac + shift_c)

    def window_idx(w, a, n):
        row, col = window_rows(w, lax.broadcasted_iota(jnp.int32, (n, 1), 0) + a)
        owner, line = split_by(row, lines)
        return (owner ^ tp) * IR + line * SIDE + col

    def slot_rows(owner, k):
        line, col = split_by(k, SIDE)
        return owner * lines + line, col

    def slot_inv(s, k):
        row, col = slot_rows(s ^ tp, k)
        wr, ar = split_by(wrap(row + SIDE - shift_r), WIN)
        wc, ac = split_by(wrap(col + SIDE - shift_c), WIN)
        return jnp.where(k < image_shard, (wr * GRID + wc) * AREA + ar * WIN + ac, -1)

    def prep_valid():
        k = lax.broadcasted_iota(jnp.int32, (IR, 1), 0)
        r.valid_i[...] = jnp.where(counts(*slot_rows(tp, k)) & (k < image_shard), 1.0, 0.0)
        n = lax.broadcasted_iota(jnp.int32, (TR, 1), 0)
        r.valid_t[...] = jnp.where(tp * TR + n < length, 1.0, 0.0)
        j = lax.broadcasted_iota(jnp.int32, (1, IP), 1)
        slot = sum((j >= s * IR).astype(jnp.int32) for s in range(1, 4))
        k = j - slot * IR
        r.cvalid[...] = jnp.where(counts(*slot_rows(slot ^ tp, k)) & (k < image_shard), 1.0, 0.0)

    def text_mask():
        def place(n):
            slot = lax.shift_right_logical(n * ((1 << 14) // TR), 14)
            return ((slot ^ tp) - slot) * TR + n

        at_q = place(lax.broadcasted_iota(jnp.int32, (TP, TP), 0))
        at_k = place(lax.broadcasted_iota(jnp.int32, (TP, TP), 1))
        return (at_k <= at_q) & (at_k < length)

    def prep_gains():
        rows = [r.gain_window, r.gain_text, r.gain_cross, r.gain_memory, r.gain_mlp]
        rows = jnp.concatenate([a[...].reshape(1, D) for a in rows] + [jnp.ones((3, D), F32)], 0)
        r.gcols[...] = jnp.swapaxes(rows, 0, 1)

    CH = [(i * (IR // 3), IR // 3) for i in range(3)] if IR % 48 == 0 else [(0, IR)]

    def ag_send(X, lo, n):
        src = X.at[0, pl.ds(lo, n)]
        return (
            push(src, X.at[2, pl.ds(lo, n)], yp),
            push(src, X.at[1, pl.ds(lo, n)], core),
            lo,
            n,
        )

    def ag_relay(X, sends):
        out = []
        for over, _, lo, n in sends:
            over.wait_recv()
            out.append(push(X.at[2, pl.ds(lo, n)], X.at[3, pl.ds(lo, n)], core))
        return out

    def wait_all(cps):
        for cp in cps:
            cp.wait_recv()

    def tag(T):
        return [push(T.at[0], T.at[i + 1], peers[i]) for i in range(3)]

    def trs_send(i, part):
        r.OT[i] = part[0:TR]
        for s in range(1, 4):
            r.TS[i, s - 1] = part[s * TR : (s + 1) * TR].astype(BF)
        return [push(r.TS.at[i, s], r.TR.at[i, s], peers[s]) for s in range(3)]

    def trs_sum(i, cps):
        wait_all(cps)
        tot = r.OT[i]
        for s in range(3):
            tot = tot + r.TR[i, s].astype(F32)
        return tot

    TILE = 256 if D % 256 == 0 else D
    NT_ = D // TILE

    last_rs = {}

    def rs_start(b, partial):
        S3, S2, RC3, RC1, RY = (r.RB.at[b, i] for i in range(5))
        S1 = S3

        def fill(slot, dst, add=None):
            def step(t, _):
                cols = pl.ds(pl.multiple_of(t * TILE, TILE), TILE)
                v = partial(slot, t, cols)
                if add is not None:
                    v = v + add[:, cols].astype(F32)
                dst[:, cols] = v.astype(dst.dtype)
                return 0

            lax.fori_loop(0, NT_, step, 0)

        st = SimpleNamespace(b=b, c1=[], cy=[])
        if b in last_rs:
            sent(last_rs[b].c1 + last_rs[b].cy)
        last_rs[b] = st
        fill(3, S3)
        c3 = [push(S3.at[pl.ds(lo, n)], RC3.at[pl.ds(lo, n)], core) for lo, n in CH]
        yield st
        fill(2, S2)
        wait_all(c3)

        def addup(t, _):
            cols = pl.ds(pl.multiple_of(t * TILE, TILE), TILE)
            S2[:, cols] = (S2[:, cols].astype(F32) + RC3[:, cols].astype(F32)).astype(BF)
            return 0

        lax.fori_loop(0, NT_, addup, 0)
        st.cy = [push(S2.at[pl.ds(lo, n)], RY.at[pl.ds(lo, n)], yp) for lo, n in CH]
        yield st
        sent(c3)
        fill(1, S1)
        st.c1 = [push(S1.at[pl.ds(lo, n)], RC1.at[pl.ds(lo, n)], core) for lo, n in CH]
        yield st
        fill(0, r.OB.at[b])
        yield st

    def rs_sum(st, i):
        lo, n = CH[i]
        st.c1[i].wait_recv()
        st.cy[i].wait_recv()
        rows = pl.ds(lo, n)
        return (
            r.OB[st.b, rows]
            + r.RB[st.b, 3, rows].astype(F32)
            + r.RB[st.b, 4, rows].astype(F32)
        )

    gx, gzc = {}, {}

    def g_start(g):
        if not fused:
            return
        gx[g] = [
            push(r.W.at[g, rows_of(zid(d) * 2 + (1 - x))], r.XR.at[g, d], xpeer)
            for d in [*range(1, nz), 0]
        ]

    def g_mid(g):
        if not fused:
            return
        gzc[g] = []
        for i, d in enumerate([*range(1, nz), 0]):
            gx[g][i].wait_recv()
            if d == 0:
                continue
            at = rows_of(zid(d) * 2 + x)
            r.W[g, at] = (r.W[g, at].astype(F32) + r.XR[g, d].astype(F32)).astype(BF)
            gzc[g].append(push(r.W.at[g, at], r.ZR.at[g, d - 1], zpeer(d)))

    def put_grad(g, tot):
        if g < 3:
            qkv, out = ((r.g_window, r.g_window_out), (r.g_text, r.g_text_out), (r.g_cross, r.g_cross_out))[g]
            for j in range(3):
                qkv[j] = tot[:, j * wd : (j + 1) * wd]
            out[...] = jnp.swapaxes(tot[:, 3 * wd :], 0, 1)
        else:
            (r.g_up, r.g_down)[g - 3][...] = tot

    def put_gains(tot):
        outs = (r.gg_window, r.gg_text, r.gg_cross, r.gg_memory, r.gg_mlp)
        for k, out in enumerate(outs):
            out[...] = tot[k : k + 1].reshape(D)

    def g_fin(g):
        if not fused:
            return
        wait_all(gzc[g])
        tot = r.W[g, rows_of(sq)].astype(F32) + r.XR[g, 0].astype(F32)
        for d in range(nz - 1):
            tot = tot + r.ZR[g, d].astype(F32)
        put_grad(g, tot)

    GT = 128
    NG = D // GT

    def gain_col(k, lo):
        return r.gcols[pl.ds(lo, GT), :][:, k : k + 1]

    def add_gain(k, lo, prod, first):
        lane = lax.broadcasted_iota(jnp.int32, (GT, 128), 1)
        col = jnp.sum(prod, -1, keepdims=True)
        rows = pl.ds(lo, GT)
        r.GA[rows] = r.GA[rows] + jnp.where(lane == k, col, 0.0)

    def grads_attn(g, gains, parts):
        def step(i, _):
            lo = pl.multiple_of(i * GT, GT)
            cols = pl.ds(lo, GT)
            rows = pl.ds(lo, GT)
            gs = [p(cols) for p in parts]
            old = r.W[g, rows].astype(F32)
            full = jnp.concatenate(gs, 1)
            lane = lax.broadcasted_iota(jnp.int32, (GT, D), 1)
            prod = full * old
            scale = jnp.ones((GT, D), F32)
            at = 0
            for k, width in gains:
                sel = (lane >= at) & (lane < at + width)
                add_gain(k, lo, jnp.where(sel, prod, 0.0), False)
                scale = jnp.where(sel, gain_col(k, lo), scale)
                at += width
            r.W[g, rows] = (full * scale).astype(BF)
            return 0

        lax.fori_loop(0, NG, step, 0)

    def prep_attn(g, ks):
        def step(i, _):
            lo = pl.multiple_of(i * GT, GT)
            rows = pl.ds(lo, GT)
            w = r.W[g, rows].astype(F32)
            for j in range(4):
                part = w[:, j * wd : (j + 1) * wd]
                if ks[j] is not None:
                    part = part * gain_col(ks[j], lo)
                r.PW[g, j, rows] = part.astype(BF)
            return 0

        lax.fori_loop(0, NG, step, 0)

    for cp in first:
        cp.wait()
    for i, buf in enumerate((r.MID, r.GM)):
        buf[cut:IR] = jnp.zeros((IR - cut, D), F32)
        buf[cut:image_shard] = r.TL[i]
    ag1 = []
    for lo, n in CH:
        rows = pl.ds(lo, n)
        xh, rstd = ln_fwd(r.MID[rows])
        r.XH1[rows] = xh
        r.RS1[rows] = rstd
        r.X1[0, rows] = xh.astype(BF)
        ag1.append(ag_send(r.X1, lo, n))
    xh, rstd = ln_fwd(r.text[...])
    r.XHA[...] = xh
    r.RSA[...] = rstd
    r.X1T[0] = xh.astype(BF)
    tag1 = tag(r.X1T)
    prep_valid()
    prep_gains()
    r.GA[...] = jnp.zeros_like(r.GA)
    for lo, n in CH:
        rows = pl.ds(lo, n)
        r.DY[0, rows] = (r.GM[rows] * r.valid_i[rows]).astype(BF)
    r.DYT[0] = (r.tcot[...] * r.valid_t[...]).astype(BF)
    if fused:
        for g in range(1, 5):
            w_pack(g)
    w_relay(0)
    w_send(1)
    rel1 = ag_relay(r.X1, ag1)
    agdy = [ag_send(r.DY, lo, n) for lo, n in CH]
    tagdy = tag(r.DYT)
    if not fused:
        for cp in local:
            cp.wait()
    w_ready(0)
    prep_attn(0, (0, 0, 0, None))
    w_relay(1)
    w_send(2)

    def qkv_slot(s):
        def step(j, _):
            v = nn(r.X1[s], r.PW[0, j]) * jnp.where(j == 0, SCALE, 1.0)
            r.QR[j, pl.ds(s * IR, IR)] = v.astype(BF)
            return 0

        lax.fori_loop(0, 3, step, 0)

    qkv_slot(0)
    wait_all([a[1] for a in ag1])
    qkv_slot(1)
    qkv_slot(2)
    wait_all(rel1)
    qkv_slot(3)
    reldy = ag_relay(r.DY, agdy)

    WG = 3 * AREA

    def perm_chunk(i):
        n = 16

        def build(t, _):
            lo = pl.multiple_of(t * n, n)
            w, a = i * 3 + t // (AREA // n), t % (AREA // n) * n
            hit = window_idx(w, a, n) == lax.broadcasted_iota(jnp.int32, (n, IP), 1)
            r.PB[pl.ds(lo, n)] = jnp.where(hit, 1.0, 0.0).astype(BF)
            return 0

        lax.fori_loop(0, WG // n, build, 0)
        return pl.ds(pl.multiple_of(i * WG, WG), WG)

    def perm_q(i, _):
        dst = perm_chunk(i)

        def step(j, _):
            r.QW[j, dst] = nn(r.PB[...], r.QR[j]).astype(BF)
            return 0

        return lax.fori_loop(0, 3, step, 0)

    lax.fori_loop(0, 3, perm_q, 0)

    def win_fwd(w, _):
        at = pl.ds(pl.multiple_of(w * AREA, AREA), AREA)
        i0 = lax.broadcasted_iota(jnp.int32, (AREA, AREA), 0)
        i1 = lax.broadcasted_iota(jnp.int32, (AREA, AREA), 1)
        good = counts(*window_rows(w, lax.broadcasted_iota(jnp.int32, (1, AREA), 1)))
        ok = jnp.where(i0 == i1, 1.0, jnp.where(good, 1.0, 0.0))
        ok = jnp.concatenate([ok] * len(masks), 0) > 0.0
        o, p = attend(r.QW[0, at], r.QW[1, at], r.QW[2, at], ok, masks)
        r.AW[at] = o
        r.PWIN[w] = p
        return 0

    lax.fori_loop(0, COUNT, win_fwd, 0)
    w_ready(1)
    w_relay(2)
    w_send(3)
    prep_attn(1, (1, 1, 1, None))

    def inv_chunk(s):
        n = 16

        def build(t, _):
            lo = pl.multiple_of(t * n, n)
            k = lax.broadcasted_iota(jnp.int32, (n, 1), 0) + lo
            hit = slot_inv(s, k) == lax.broadcasted_iota(jnp.int32, (n, COUNT * AREA), 1)
            r.PTB[pl.ds(lo, n)] = jnp.where(hit, 1.0, 0.0).astype(BF)
            return 0

        lax.fori_loop(0, IR // n, build, 0)

    def attn_rows(s, _):
        inv_chunk(s)
        r.AR[s] = nn(r.PTB[...], r.AW[...]).astype(BF)
        return 0

    lax.fori_loop(0, 4, attn_rows, 0)

    def wtile(g, j, cols):
        return r.PW[g, j, cols]

    rs1 = rs_start(0, lambda s, t, cols: nt(r.AR[s], wtile(0, 3, cols)))
    next(rs1)
    next(rs1)

    wait_all(tag1)
    xt = r.X1T[...].reshape(TP, D)
    r.TQ[0] = (nn(xt, r.PW[1, 0]) * SCALE).astype(BF)
    r.TQ[1] = nn(xt, r.PW[1, 1]).astype(BF)
    r.TQ[2] = nn(xt, r.PW[1, 2]).astype(BF)
    ok_t = jnp.concatenate([jnp.where(text_mask(), 1.0, 0.0)] * len(masks), 0) > 0.0
    o, p = attend(r.TQ[0], r.TQ[1], r.TQ[2], ok_t, masks)
    r.TA[...] = o
    r.TPR[...] = p
    trs1 = trs_send(0, nt(r.TA[...], r.PW[1, 3]))
    next(rs1)
    st1 = next(rs1)
    w_ready(2)
    w_relay(3)
    w_send(4)
    prep_attn(2, (2, 3, 3, None))

    tmid = r.text[...] + r.valid_t[...] * trs_sum(0, trs1)
    r.TMID[...] = tmid
    xh, rstd = ln_fwd(tmid)
    r.XHQ[...] = xh
    r.RSQ[...] = rstd
    r.X2T[0] = xh.astype(BF)
    tag2 = tag(r.X2T)
    ag2 = []
    for i, (lo, n) in enumerate(CH):
        rows = pl.ds(lo, n)
        mid = r.MID[rows] + r.valid_i[rows] * rs_sum(st1, i)
        r.MID[rows] = mid
        xh, rstd = ln_fwd(mid)
        r.XH2[rows] = xh
        r.RS2[rows] = rstd
        r.X2[0, rows] = xh.astype(BF)
        ag2.append(ag_send(r.X2, lo, n))
    wait_all([a[1] for a in agdy] + reldy + tagdy)
    sent([a[1] for a in agdy] + [a[0] for a in agdy] + reldy)

    def kv_slot(s):
        def step(j, _):
            r.KV[j, pl.ds(s * IR, IR)] = nn(r.X2[s], r.PW[2, j + 1]).astype(BF)
            return 0

        lax.fori_loop(0, 2, step, 0)

    kv_slot(0)
    wait_all(tag2)
    r.CQ[...] = (nn(r.X2T[...].reshape(TP, D), r.PW[2, 0]) * SCALE).astype(BF)
    w_ready(3)
    w_relay(4)

    def prep_up(i, _):
        lo = pl.multiple_of(i * GT, GT)
        rows = pl.ds(lo, GT)
        r.W[3, rows] = (r.W[3, rows].astype(F32) * gain_col(4, lo)).astype(BF)
        return 0

    lax.fori_loop(0, NG, prep_up, 0)
    wait_all([a[1] for a in ag2])
    kv_slot(1)
    rel2 = ag_relay(r.X2, ag2)
    kv_slot(2)
    wait_all(rel2)
    kv_slot(3)

    def head(h):
        lane = lax.broadcasted_iota(jnp.int32, (1, wd), 1)
        return jnp.where((lane >= h * HD) & (lane < (h + 1) * HD), 1.0, 0.0).astype(BF)

    def cross_head(h, _):
        rows = pl.ds(pl.multiple_of(h * TP, TP), TP)
        qm = r.CQ[...] * head(h)
        s = jnp.where(r.cvalid[...] > 0.0, nt(qm, r.KV[0]), NEG)
        e = jnp.exp(s - jnp.max(s, -1, keepdims=True))
        r.CP[rows] = (e * (1.0 / jnp.sum(e, -1, keepdims=True))).astype(BF)
        return 0

    lax.fori_loop(0, len(masks), cross_head, 0)
    r.CA[...] = merge_heads(nn(r.CP[...], r.KV[1]), masks).astype(BF)
    trs2 = trs_send(1, nt(r.CA[...], r.PW[2, 3]))
    w_ready(4)

    def mlp_tile(xb, dyb, cols):
        u = nn(xb, r.W[3, :, cols])
        th = jnp.tanh(GELU_C * (u + GELU_A * u * u * u))
        act = 0.5 * u * (1.0 + th)
        slope = 0.5 * (1.0 + th) + 0.5 * u * (1.0 - th * th) * (
            GELU_C * (1.0 + 3.0 * GELU_A * u * u)
        )
        ga = nn(dyb, r.W[4, :, cols])
        return act.astype(BF), (ga * slope).astype(BF)

    HT = 256 if hid % 256 == 0 else hid

    def mlp_slot(s):
        def step(t, _):
            cols = pl.ds(pl.multiple_of(t * HT, HT), HT)
            a, gu = mlp_tile(r.X2[s], r.DY[s], cols)
            r.ACT[s, :, cols] = a
            r.GU[s, :, cols] = gu
            return 0

        lax.fori_loop(0, hid // HT, step, 0)

    rs2 = rs_start(1, lambda s, t, cols: nt(r.ACT[s], r.W[4, cols]))
    mlp_slot(3)
    next(rs2)
    tlate = r.TMID[...] + r.valid_t[...] * trs_sum(1, trs2)
    r.TMID[...] = tlate
    xh, rstd = ln_fwd(tlate)
    r.XHL[...] = xh
    r.RSL[...] = rstd
    r.XT[0] = xh.astype(BF)
    tag3 = tag(r.XT)
    mlp_slot(2)
    next(rs2)
    wait_all(tag3)

    def mlp_text(t, _):
        cols = pl.ds(pl.multiple_of(t * HT, HT), HT)
        a, gu = mlp_tile(r.XT[...].reshape(TP, D), r.DYT[...].reshape(TP, D), cols)
        r.ACTT[:, cols] = a
        r.GUT[:, cols] = gu
        return 0

    lax.fori_loop(0, hid // HT, mlp_text, 0)
    trs4 = trs_send(3, nt(r.GUT[...], r.W[3]))
    trs3 = trs_send(2, nt(r.ACTT[...], r.W[4]))
    mlp_slot(1)
    next(rs2)
    gtl = r.tcot[...] + ln_bwd(trs_sum(3, trs4), r.XHL[...], r.RSL[...])
    r.GTX[...] = gtl
    r.DC[0] = (gtl * r.valid_t[...]).astype(BF)
    tag4 = tag(r.DC)
    mlp_slot(0)
    st2 = next(rs2)

    wait_all(tag4)
    da = nn(r.DC[...].reshape(TP, D), r.PW[2, 3]).astype(BF)
    das = stack_heads(da, masks)
    r.CDA[...] = da

    def cross_head_back(h, _):
        rows = pl.ds(pl.multiple_of(h * TP, TP), TP)
        dp = nt(r.CDA[...] * head(h), r.KV[1])
        pf = r.CP[rows].astype(F32)
        pd = pf * dp
        r.PB[rows] = (pd - pf * jnp.sum(pd, -1, keepdims=True)).astype(BF)
        return 0

    lax.fori_loop(0, len(masks), cross_head_back, 0)
    HR = len(masks) * TP
    ds = r.PB[0:HR]
    r.CDQ[...] = (merge_heads(nn(ds, r.KV[0]), masks) * SCALE).astype(BF)
    r.DKV[0] = tn(ds, stack_heads(r.CQ[...], masks)).astype(BF)
    r.DKV[1] = tn(r.CP[...], das).astype(BF)
    trs5 = trs_send(4, nt(r.CDQ[...], r.PW[2, 0]))

    def gd_step(i, _):
        lo = pl.multiple_of(i * GT, GT)
        cols = pl.ds(lo, GT)
        full = tn(r.DY[:, :, cols].reshape(IP, GT), r.ACT[...].reshape(IP, hid))
        full = full + tn(r.DYT[:, :, cols].reshape(TP, GT), r.ACTT[...])
        r.W[4, pl.ds(lo, GT)] = full.astype(BF)
        return 0

    lax.fori_loop(0, NG, gd_step, 0)
    g_start(4)

    def mid_partial(s, t, cols):
        at = pl.ds(s * IR, IR)
        return (
            nt(r.GU[s], r.W[3, cols])
            + nt(r.DKV[0, at], wtile(2, 1, cols))
            + nt(r.DKV[1, at], wtile(2, 2, cols))
        )

    rs3 = rs_start(0, mid_partial)
    for _ in range(4):
        st3 = next(rs3)

    def gu_step(i, _):
        lo = pl.multiple_of(i * GT, GT)
        cols = pl.ds(lo, GT)
        rows = pl.ds(lo, GT)
        full = tn(r.X2[:, :, cols].reshape(IP, GT), r.GU[...].reshape(IP, hid))
        full = full + tn(r.XT[:, :, cols].reshape(TP, GT), r.GUT[...])
        add_gain(4, lo, full * r.W[3, rows].astype(F32) * (1.0 / gain_col(4, lo)), False)
        r.W[3, rows] = (full * gain_col(4, lo)).astype(BF)
        return 0

    lax.fori_loop(0, NG, gu_step, 0)
    g_start(3)

    gtm = r.GTX[...] + ln_bwd(trs_sum(4, trs5), r.XHQ[...], r.RSQ[...])
    r.GTX[...] = gtm
    r.DWT[0] = (gtm * r.valid_t[...]).astype(BF)
    tag5 = tag(r.DWT)

    for i in range(len(CH)):
        lo, n = CH[i]
        rows = pl.ds(lo, n)
        r.MID[rows] = r.MID[rows] + r.valid_i[rows] * rs_sum(st2, i)
    out_i = rows_out(0, r.MID, r.image_out)
    r.text_out[0] = r.TMID[...] + r.valid_t[...] * trs_sum(2, trs3)

    ag3 = []
    for i, (lo, n) in enumerate(CH):
        rows = pl.ds(lo, n)
        gm = r.GM[rows] + ln_bwd(rs_sum(st3, i), r.XH2[rows], r.RS2[rows])
        r.GM[rows] = gm
        r.DY[0, rows] = (gm * r.valid_i[rows]).astype(BF)
        ag3.append(ag_send(r.DY, lo, n))

    grads_attn(
        2,
        ((2, wd), (3, 2 * wd)),
        (
            lambda cols: tn(r.X2T[:, :, cols].reshape(TP, GT), r.CDQ[...]),
            lambda cols: tn(r.X2[:, :, cols].reshape(IP, GT), r.DKV[0]),
            lambda cols: tn(r.X2[:, :, cols].reshape(IP, GT), r.DKV[1]),
            lambda cols: tn(r.DC[:, :, cols].reshape(TP, GT), r.CA[...]),
        ),
    )
    g_start(2)
    g_mid(4)

    wait_all(tag5)
    da = nn(r.DWT[...].reshape(TP, D), r.PW[1, 3]).astype(BF)
    dq, dk, dv = attend_back(r.TQ[0], r.TQ[1], r.TQ[2], r.TPR[...], da, masks)
    r.DTQ[0] = dq
    r.DTQ[1] = dk
    r.DTQ[2] = dv
    trs6 = trs_send(
        5,
        nt(r.DTQ[0], r.PW[1, 0]) + nt(r.DTQ[1], r.PW[1, 1]) + nt(r.DTQ[2], r.PW[1, 2]),
    )
    rel3 = ag_relay(r.DY, ag3)

    def da_slot(s):
        r.DKV[0, pl.ds(s * IR, IR)] = nn(r.DY[s], r.PW[0, 3]).astype(BF)

    da_slot(0)
    wait_all([a[1] for a in ag3])
    da_slot(1)
    da_slot(2)
    grads_attn(
        1,
        ((1, 3 * wd),),
        tuple(
            (lambda cols, j=j: tn(r.X1T[:, :, cols].reshape(TP, GT), r.DTQ[j]))
            for j in range(3)
        )
        + (lambda cols: tn(r.DWT[:, :, cols].reshape(TP, GT), r.TA[...]),),
    )
    g_start(1)
    g_mid(3)
    wait_all(rel3)
    da_slot(3)

    def perm_d(i, _):
        dst = perm_chunk(i)
        r.AW[dst] = nn(r.PB[...], r.DKV[0]).astype(BF)
        return 0

    lax.fori_loop(0, 3, perm_d, 0)

    def win_bwd(w, _):
        at = pl.ds(pl.multiple_of(w * AREA, AREA), AREA)
        dq, dk, dv = attend_back(
            r.QW[0, at], r.QW[1, at], r.QW[2, at], r.PWIN[w], r.AW[at], masks
        )
        r.QW[0, at] = dq
        r.QW[1, at] = dk
        r.QW[2, at] = dv
        return 0

    lax.fori_loop(0, COUNT, win_bwd, 0)
    g_mid(2)

    def back_rows(s):
        inv_chunk(s)

        def step(j, _):
            r.QR[j, pl.ds(s * IR, IR)] = nn(r.PTB[...], r.QW[j]).astype(BF)
            return 0

        lax.fori_loop(0, 3, step, 0)

    def win_partial(s, t, cols):
        at = pl.ds(s * IR, IR)
        return (
            nt(r.QR[0, at], wtile(0, 0, cols))
            + nt(r.QR[1, at], wtile(0, 1, cols))
            + nt(r.QR[2, at], wtile(0, 2, cols))
        )

    rs4 = rs_start(1, win_partial)
    back_rows(3)
    next(rs4)
    back_rows(2)
    next(rs4)
    back_rows(1)
    back_rows(0)
    grads_attn(
        0,
        ((0, 3 * wd),),
        tuple(
            (lambda cols, j=j: tn(r.X1[:, :, cols].reshape(IP, GT), r.QR[j]))
            for j in range(3)
        )
        + (
            lambda cols: tn(r.DY[:, :, cols].reshape(IP, GT), r.AR[...].reshape(IP, wd)),
        ),
    )
    g_start(0)
    next(rs4)
    st4 = next(rs4)
    g_mid(1)

    r.GB[0] = jnp.swapaxes(r.GA[...], 0, 1)[0:8]
    gc = push(r.GB.at[0], r.GR.at[0], core)
    r.text_grad[0] = r.GTX[...] + ln_bwd(trs_sum(5, trs6), r.XHA[...], r.RSA[...])
    gc.wait_recv()
    r.GB[1] = r.GB[0] + r.GR[0]
    gc = push(r.GB.at[1], r.GR.at[1], yp)
    g_fin(4)
    gc.wait_recv()
    if fused:
        r.GB[2] = r.GB[1] + r.GR[1]
        gc = push(r.GB.at[2], r.GR.at[2], xpeer)
        g_mid(0)
        gc.wait_recv()
        r.GZ[z] = r.GB[2] + r.GR[2]
        gcs = [
            push(r.GZ.at[z], r.GZ.at[z], zpeer(d), r.GZ.at[zback(d)]) for d in range(1, nz)
        ]
    for i, (lo, n) in enumerate(CH):
        rows = pl.ds(lo, n)
        r.GM[rows] = r.GM[rows] + ln_bwd(rs_sum(st4, i), r.XH1[rows], r.RS1[rows])
    out_g = rows_out(1, r.GM, r.image_grad)
    g_fin(3)
    g_fin(2)
    g_fin(1)
    if fused:
        wait_all(gcs)
        tot = r.GZ[0]
        for d in range(1, nz):
            tot = tot + r.GZ[d]
        put_gains(tot)
    else:
        put_gains(r.GB[1] + r.GR[1])
    g_fin(0)
    if not fused:
        for g in range(5):
            cp = pltpu.make_async_copy(r.W.at[g], r.G_out.at[g], r.lsem.at[g])
            cp.start()
            cp.wait()
    for cp in out_i + out_g:
        cp.wait()
    for cp in pending:
        cp.wait_send()
    assert counter[0] <= NSEM


def run_kernel(cfg, inputs):
    D, wd, hid, IR, TR, nz, sr, fused = (
        cfg.D, cfg.wd, cfg.hid, cfg.IR, cfg.TR, cfg.nz, cfg.sr, cfg.fused,
    )
    IP, TP = 4 * IR, 4 * TR
    NH = wd // HD
    ROWS = COUNT * AREA
    vm = pl.BlockSpec(memory_space=pltpu.VMEM)
    hbm = pl.BlockSpec(memory_space=pl.ANY)
    scalars = ("page_dims", "shifts", "text_length")
    in_names = list(inputs)
    smem = pl.BlockSpec(memory_space=pltpu.SMEM)
    in_specs = [
        hbm if n in ("wfull", "image", "icot") else smem if n in scalars else vm for n in in_names
    ]
    outs = [
        ("image_out", (cfg.image_shard, 1, D), F32, hbm),
        ("text_out", (1, TR, D), F32, vm),
        ("image_grad", (cfg.image_shard, 1, D), F32, hbm),
        ("text_grad", (1, TR, D), F32, vm),
    ]
    if fused:
        for n in ("window", "text", "cross"):
            outs += [("g_" + n, (3, sr, wd), F32, vm), ("g_" + n + "_out", (wd, sr), F32, vm)]
        outs += [("g_up", (sr, hid), F32, vm), ("g_down", (sr, hid), F32, vm)]
    else:
        outs += [("G_out", (5, D, D), BF, hbm)]
    outs += [("gg_" + n, (D,), F32, vm) for n in ("window", "text", "cross", "memory", "mlp")]
    V = pltpu.VMEM
    scratch = {
        "W": V((5, D, D), BF),
        "PW": V((3, 4, D, wd), BF),
        "X1": V((4, IR, D), BF),
        "X2": V((4, IR, D), BF),
        "DY": V((4, IR, D), BF),
        "X1T": V((4, TR, D), BF),
        "X2T": V((4, TR, D), BF),
        "XT": V((4, TR, D), BF),
        "DYT": V((4, TR, D), BF),
        "DC": V((4, TR, D), BF),
        "DWT": V((4, TR, D), BF),
        "MID": V((IR, D), F32),
        "GM": V((IR, D), F32),
        "XH1": V((IR, D), F32),
        "XH2": V((IR, D), F32),
        "RS1": V((IR, 1), F32),
        "RS2": V((IR, 1), F32),
        "TMID": V((TR, D), F32),
        "GTX": V((TR, D), F32),
        "XHA": V((TR, D), F32),
        "XHQ": V((TR, D), F32),
        "XHL": V((TR, D), F32),
        "RSA": V((TR, 1), F32),
        "RSQ": V((TR, 1), F32),
        "RSL": V((TR, 1), F32),
        "QR": V((3, IP, wd), BF),
        "QW": V((3, ROWS, wd), BF),
        "PWIN": V((COUNT, NH * AREA, AREA), BF),
        "AW": V((ROWS, wd), BF),
        "AR": V((4, IR, wd), BF),
        "KV": V((2, IP, wd), BF),
        "DKV": V((2, IP, wd), BF),
        "CQ": V((TP, wd), BF),
        "CDQ": V((TP, wd), BF),
        "CDA": V((TP, wd), BF),
        "CA": V((TP, wd), BF),
        "CP": V((NH * TP, IP), BF),
        "TQ": V((3, TP, wd), BF),
        "DTQ": V((3, TP, wd), BF),
        "TA": V((TP, wd), BF),
        "TPR": V((NH * TP, TP), BF),
        "ACT": V((4, IR, hid), BF),
        "GU": V((4, IR, hid), BF),
        "ACTT": V((TP, hid), BF),
        "GUT": V((TP, hid), BF),
        "PB": V((3 * AREA, IP), BF),
        "PTB": V((IR, ROWS), BF),
        "RB": V((2, 5, IR, D), BF),
        "OB": V((2, IR, D), F32),
        "TS": V((6, 3, TR, D), BF),
        "TR": V((6, 3, TR, D), BF),
        "OT": V((6, TR, D), F32),
        "GA": V((D, 128), F32),
        "GB": V((3, 8, D), F32),
        "GR": V((3, 8, D), F32),
        "valid_i": V((IR, 1), F32),
        "valid_t": V((TR, 1), F32),
        "cvalid": V((1, IP), F32),
        "gcols": V((D, 8), F32),
        "ssem": pltpu.SemaphoreType.DMA((NSEM,)),
        "rsem": pltpu.SemaphoreType.DMA((NSEM,)),
        "TL": V((2, cfg.image_shard % 8, D), F32),
        "lsem": pltpu.SemaphoreType.DMA((9,)),
    }
    if fused:
        scratch |= {
            "XR": V((5, nz, sr, D), BF),
            "ZR": V((5, max(nz - 1, 1), sr, D), BF),
            "GZ": V((nz, 8, D), F32),
        }
    cfg.names = in_names + [o[0] for o in outs] + list(scratch)
    return pl.pallas_call(
        functools.partial(kernel, cfg),
        out_shape=[jax.ShapeDtypeStruct(o[1], o[2]) for o in outs],
        in_specs=in_specs,
        out_specs=[o[3] for o in outs],
        scratch_shapes=list(scratch.values()),
        compiler_params=pltpu.CompilerParams(
            collective_id=0, has_side_effects=True, vmem_limit_bytes=int(63.25 * 1024 * 1024)
        ),
    )(*[inputs[n] for n in in_names])


def body(
    n_seq,
    image_in, text_in, w_window, w_window_out, w_text, w_text_out, w_cross, w_cross_out,
    w_up, w_down, gain_window, gain_text, gain_cross, gain_memory, gain_mlp,
    page_dims, shifts, text_length, image_cotan, text_cotan,
):
    D = image_in.shape[-1]
    wd = w_window.shape[-1]
    hid = w_up.shape[-1]
    sr = w_up.shape[0]
    shard = image_in.shape[1]
    TR = text_in.shape[1]
    IR = -(-shard // 16) * 16
    me = lax.axis_index("tp")
    fused = n_seq % 2 == 0 and sr % 16 == 0
    cfg = SimpleNamespace(
        D=D, wd=wd, hid=hid, IR=IR, TR=TR, nz=n_seq // 2, sr=sr, fused=fused, image_shard=shard
    )

    cut = shard // 8 * 8
    assert D == 4 * wd and D == hid and shard % SIDE == 0 and cut < shard
    inputs = {
        "image": image_in.transpose(1, 0, 2),
        "text": text_in[0],
        "icot": image_cotan.transpose(1, 0, 2),
        "tcot": text_cotan[0],
        "page_dims": page_dims,
        "shifts": shifts,
        "text_length": text_length,
        "gain_window": gain_window,
        "gain_text": gain_text,
        "gain_cross": gain_cross,
        "gain_memory": gain_memory,
        "gain_mlp": gain_mlp,
    }
    if fused:
        inputs |= {
            "w_window": w_window,
            "w_window_out": w_window_out,
            "w_text": w_text,
            "w_text_out": w_text_out,
            "w_cross": w_cross,
            "w_cross_out": w_cross_out,
            "w_up": w_up,
            "w_down": w_down.T,
        }
    else:

        def pack(w, out):
            return jnp.concatenate([w[0], w[1], w[2], out.T], 1)

        packed = [
            pack(w_window, w_window_out),
            pack(w_text, w_text_out),
            pack(w_cross, w_cross_out),
            w_up,
            w_down.T,
        ]
        inputs["wfull"] = lax.all_gather(jnp.stack(packed), "seq", axis=1, tiled=True)
    outs = run_kernel(cfg, inputs)
    if fused:
        outs = copy_out(outs)
    rows, gains = outs[:4], outs[-5:]
    if fused:
        grads = outs[4:-5]
    else:
        G = lax.psum_scatter(outs[4].astype(F32), "seq", scatter_dimension=1, tiled=True)
        gains = [lax.psum(g, "seq") for g in gains]
        grads = []
        for g in G[:3]:
            grads += [g[:, : 3 * wd].reshape(sr, 3, wd).transpose(1, 0, 2), g[:, 3 * wd :].T]
        grads += [G[3], G[4]]
    image_out, text_out, image_grad, text_grad = rows
    return (
        image_out.transpose(1, 0, 2), text_out, image_grad.transpose(1, 0, 2), text_grad,
        *grads[:7], grads[7].T, *gains,
    )


def copy_out(arrays):
    n = len(arrays)

    def copies(*refs):
        sem, held = refs[2 * n], refs[2 * n + 1 :]
        into = [pltpu.make_async_copy(refs[i], held[i], sem.at[i]) for i in range(n)]
        out = [pltpu.make_async_copy(held[i], refs[n + i], sem.at[n + i]) for i in range(n)]
        for cp in into:
            cp.start()
        for i in range(n):
            into[i].wait()
            out[i].start()
        for cp in out:
            cp.wait()

    return pl.pallas_call(
        copies,
        out_shape=[jax.ShapeDtypeStruct(a.shape, a.dtype) for a in arrays],
        in_specs=[pl.BlockSpec(memory_space=pl.ANY)] * n,
        out_specs=[pl.BlockSpec(memory_space=pl.ANY)] * n,
        scratch_shapes=[pltpu.SemaphoreType.DMA((2 * n,))]
        + [pltpu.VMEM(a.shape, a.dtype) for a in arrays],
        compiler_params=pltpu.CompilerParams(vmem_limit_bytes=60 * 1024 * 1024),
    )(*arrays)


def solution(mesh):
    rows = P("seq", "tp", None)
    qkv = P(None, "seq", "tp")
    out = P("tp", "seq")
    return jax.shard_map(
        functools.partial(body, mesh.shape["seq"]),
        mesh=mesh,
        in_specs=(
            rows, rows, qkv, out, qkv, out, qkv, out, P("seq", "tp"), out,
            P(), P(), P(), P(), P(), P("seq", None), P("seq", None), P("seq"), rows, rows,
        ),
        out_specs=(
            rows, rows, rows, rows, qkv, out, qkv, out, qkv, out, P("seq", "tp"), out,
            P(), P(), P(), P(), P(),
        ),
        check_vma=False,
    )
```

profile of v0, /device:TPU:9, one launch (start us, length us, event | category | flops | bytes accessed | tf_op | source)
XLA Modules:
  0.0 222.6 jit_solution(16278655444062973759)
XLA Ops:
  1.3 217.6 %shard_map.323 = (f32[324,1,768]{2,1,0:T(1,128)}, f32[1,32,768]{2,1,0:T(8,128)}, f32[324,1,768]{2,1,0:T(1,128)}, f32[1,32,768]{2,1,0:T(8,128)}, f32[3,96,192]{2,...) custom-call(f32[324,1,768]{2,1,0:T(1,128)} %bitcast.8, ...), custom_call_target="tpu_custom_call" | custom-call | tf_op jit(solution)/shard_map/pallas_call | solution.py:1068
  218.9 3.5 %shard_map.324 = (f32[324,1,768]{2,1,0:T(1,128)}, f32[1,32,768]{2,1,0:T(8,128)}, f32[324,1,768]{2,1,0:T(1,128)}, f32[1,32,768]{2,1,0:T(8,128)}, f32[3,96,192]{2,...) custom-call(f32[324,1,768]{2,1,0:T(1,128)} %get-tuple-element.51.ref, ...), custom_call_target="tpu_custom_call" | custom-call | tf_op jit(solution)/shard_map/pallas_call | solution.py:1174
where the time goes:
time: 225 us; the launch traced here: 223 us
  Pallas kernels  221 us (98%)
    pallas_call x1, Pallas kernels, run_kernel(): pl.pallas_call(functools.partial(kernel, cfg), out_shape=[jax.ShapeDtypeS...  218 us

commit v1 on v0

--- a/solution.py
+++ b/solution.py
@@ -48,46 +48,69 @@
     )
 
 
-def head_masks(width):
-    lane = lax.broadcasted_iota(jnp.int32, (1, width), 1) // HD
-    return [lane == h for h in range(width // HD)]
-
-
-def stack_heads(v, masks):
-    return jnp.concatenate(
-        [v * jnp.where(m, 1.0, 0.0).astype(BF) for m in masks], 0
-    )
-
-
-def merge_heads(v3, masks):
-    n = v3.shape[0] // len(masks)
-    out = jnp.where(masks[0], v3[:n], 0.0)
-    for h in range(1, len(masks)):
-        out = out + jnp.where(masks[h], v3[h * n : (h + 1) * n], 0.0)
+def head_lanes(width, heads, at=0):
+    lane = lax.broadcasted_iota(jnp.int32, (1, width), 1)
+    return [(lane >= at + h * HD) & (lane < at + (h + 1) * HD) for h in range(heads)]
+
+
+def stack_heads(v, lanes):
+    v = v.astype(F32)
+    return jnp.concatenate([jnp.where(m, v, 0.0) for m in lanes], 0).astype(BF)
+
+
+def merge_heads(v, lanes):
+    n = v.shape[0] // len(lanes)
+    out = jnp.where(lanes[0], v[:n], 0.0)
+    for h in range(1, len(lanes)):
+        out = out + jnp.where(lanes[h], v[h * n : (h + 1) * n], 0.0)
     return out
 
 
-def attend(q, k, v, allowed, masks):
-    s = nt(stack_heads(q, masks), k)
-    s = jnp.where(allowed, s, NEG)
+def softmax(s):
     e = jnp.exp(s - jnp.max(s, -1, keepdims=True))
-    p = (e * (1.0 / jnp.sum(e, -1, keepdims=True))).astype(BF)
-    return merge_heads(nn(p, v), masks).astype(BF), p
-
-
-def attend_back(q, k, v, p, da, masks):
-    das = stack_heads(da, masks)
-    dp = nt(das, v)
+    return (e * (1.0 / jnp.sum(e, -1, keepdims=True))).astype(BF)
+
+
+def score_back(p, dp):
     pf = p.astype(F32)
     pd = pf * dp
-    ds = (pd - pf * jnp.sum(pd, -1, keepdims=True)).astype(BF)
-    dq = (merge_heads(nn(ds, k), masks) * SCALE).astype(BF)
-    dk = tn(ds, stack_heads(q, masks)).astype(BF)
-    dv = tn(p, das).astype(BF)
-    return dq, dk, dv
+    return (pd - pf * jnp.sum(pd, -1, keepdims=True)).astype(BF)
+
+
+class Heads:
+    def __init__(self, wd):
+        self.wd = wd
+        n = wd // HD
+        self.own = head_lanes(wd, n)
+        self.first = head_lanes(2 * wd, n)
+        self.second = head_lanes(2 * wd, n, wd)
+
+    def place_first(self, v):
+        v = v.astype(F32)
+        return stack_heads(jnp.concatenate([v, jnp.zeros_like(v)], 1), self.first)
+
+    def place_second(self, v):
+        v = v.astype(F32)
+        return stack_heads(jnp.concatenate([jnp.zeros_like(v), v], 1), self.second)
+
+    def values(self, p, kv):
+        return merge_heads(nn(p, kv), self.second)[:, self.wd :].astype(BF)
+
+    def attend(self, k, kv, q, allowed):
+        p = softmax(jnp.where(allowed, nt(stack_heads(q, self.own), k), NEG))
+        return self.values(p, kv), p
+
+    def attend_back(self, k, kv, q, p, da):
+        das = self.place_second(da)
+        ds = score_back(p, nt(das, kv))
+        dq = (merge_heads(nn(ds, k), self.own) * SCALE).astype(BF)
+        both = jnp.concatenate([self.place_first(q), das], 0)
+        dkv = tn(jnp.concatenate([ds, p], 0), both).astype(BF)
+        return dkv, dq
 
 
 NSEM = 192
+UNROLL = 3
 
 
 def kernel(cfg, *refs):
@@ -98,7 +121,10 @@
     image_shard = cfg.image_shard
     IP = 4 * IR
     TP = 4 * TR
-    masks = head_masks(wd)
+    heads = Heads(wd)
+    NH = wd // HD
+    K, KV, Q = slice(0, wd), slice(0, 2 * wd), slice(2 * wd, 3 * wd)
+    KVQ = slice(0, 3 * wd)
 
     tp = lax.axis_index("tp")
     sq = lax.axis_index("seq")
@@ -150,7 +176,6 @@
         greet += [xpeer] + [zpeer(d) for d in range(1, nz)]
     for dev in greet:
         pl.semaphore_signal(barrier, inc=1, device_id=dev, device_id_type=MESH)
-    pl.semaphore_wait(barrier, len(greet))
 
     counter = [0]
     pending = []
@@ -182,20 +207,25 @@
 
     wz, wx = {}, {}
 
-    def w_send(g):
+    def w_send_x(g):
+        if fused:
+            own = r.W.at[g, rows_of(sq)]
+            wx[g] = [push(own, own, xpeer, r.W.at[g, rows_of(z * 2 + (1 - x))])]
+
+    def w_send_z(g):
+        if fused:
+            own = r.W.at[g, rows_of(sq)]
+            wz[g] = [
+                push(own, own, zpeer(d), r.W.at[g, rows_of(zback(d) * 2 + x)])
+                for d in range(1, nz)
+            ]
+
+    def w_relay(g, ds=None):
         if not fused:
             return
-        own = r.W.at[g, rows_of(sq)]
-        wz[g] = [
-            push(own, own, zpeer(d), r.W.at[g, rows_of(zback(d) * 2 + x)])
-            for d in range(1, nz)
-        ]
-        wx[g] = [push(own, own, xpeer, r.W.at[g, rows_of(z * 2 + (1 - x))])]
-
-    def w_relay(g):
-        if not fused:
-            return
-        for d in range(1, nz):
+        for d in ds or range(1, nz):
+            if d >= nz:
+                continue
             wz[g][d - 1].wait_recv()
             at = rows_of(zback(d) * 2 + x)
             wx[g].append(
@@ -212,7 +242,7 @@
     def w_pack(g):
         if g < 3:
             w, out = ((r.w_window, r.w_window_out), (r.w_text, r.w_text_out), (r.w_cross, r.w_cross_out))[g]
-            full = [w[j].astype(F32) for j in range(3)] + [jnp.swapaxes(out[...].astype(F32), 0, 1)]
+            full = [w[j].astype(F32) for j in (1, 2, 0)] + [jnp.swapaxes(out[...].astype(F32), 0, 1)]
             full = jnp.concatenate(full, 1)
         elif g == 3:
             full = r.w_up[...]
@@ -222,8 +252,10 @@
 
     if fused:
         w_pack(0)
-        w_send(0)
-    else:
+    pl.semaphore_wait(barrier, len(greet))
+    w_send_z(0)
+    w_send_x(0)
+    if not fused:
         local = [pltpu.make_async_copy(r.wfull.at[g], r.W.at[g], r.lsem.at[g]) for g in range(5)]
         for cp in local:
             cp.start()
@@ -329,45 +361,39 @@
 
     last_rs = {}
 
-    def rs_start(b, partial):
-        S3, S2, RC3, RC1, RY = (r.RB.at[b, i] for i in range(5))
-        S1 = S3
-
-        def fill(slot, dst, add=None):
-            def step(t, _):
-                cols = pl.ds(pl.multiple_of(t * TILE, TILE), TILE)
-                v = partial(slot, t, cols)
-                if add is not None:
-                    v = v + add[:, cols].astype(F32)
-                dst[:, cols] = v.astype(dst.dtype)
-                return 0
-
-            lax.fori_loop(0, NT_, step, 0)
-
+    def rs_fill(partial, slot, dst):
+        def step(t, _):
+            cols = pl.ds(pl.multiple_of(t * TILE, TILE), TILE)
+            dst[:, cols] = partial(slot, cols).astype(dst.dtype)
+            return 0
+
+        lax.fori_loop(0, NT_, step, 0)
+
+    def rs_far(b, partial):
         st = SimpleNamespace(b=b, c1=[], cy=[])
         if b in last_rs:
             sent(last_rs[b].c1 + last_rs[b].cy)
         last_rs[b] = st
-        fill(3, S3)
-        c3 = [push(S3.at[pl.ds(lo, n)], RC3.at[pl.ds(lo, n)], core) for lo, n in CH]
-        yield st
-        fill(2, S2)
-        wait_all(c3)
-
-        def addup(t, _):
-            cols = pl.ds(pl.multiple_of(t * TILE, TILE), TILE)
-            S2[:, cols] = (S2[:, cols].astype(F32) + RC3[:, cols].astype(F32)).astype(BF)
-            return 0
-
-        lax.fori_loop(0, NT_, addup, 0)
-        st.cy = [push(S2.at[pl.ds(lo, n)], RY.at[pl.ds(lo, n)], yp) for lo, n in CH]
-        yield st
-        sent(c3)
-        fill(1, S1)
+        S3, S2, RC3 = (r.RB.at[b, i] for i in range(3))
+        rs_fill(partial, 3, S3)
+        st.c3 = [push(S3.at[pl.ds(lo, n)], RC3.at[pl.ds(lo, n)], core) for lo, n in CH]
+        rs_fill(partial, 2, S2)
+        return st
+
+    def rs_over(st):
+        S2, RC3, RY = (r.RB.at[st.b, i] for i in (1, 2, 4))
+        for cp, (lo, n) in zip(st.c3, CH):
+            cp.wait_recv()
+            rows = pl.ds(lo, n)
+            S2[rows] = (S2[rows].astype(F32) + RC3[rows].astype(F32)).astype(BF)
+            st.cy.append(push(S2.at[rows], RY.at[rows], yp))
+
+    def rs_near(st, partial):
+        S1, RC1 = r.RB.at[st.b, 0], r.RB.at[st.b, 3]
+        sent(st.c3)
+        rs_fill(partial, 1, S1)
         st.c1 = [push(S1.at[pl.ds(lo, n)], RC1.at[pl.ds(lo, n)], core) for lo, n in CH]
-        yield st
-        fill(0, r.OB.at[b])
-        yield st
+        rs_fill(partial, 0, r.OB.at[st.b])
 
     def rs_sum(st, i):
         lo, n = CH[i]
@@ -405,8 +431,8 @@
     def put_grad(g, tot):
         if g < 3:
             qkv, out = ((r.g_window, r.g_window_out), (r.g_text, r.g_text_out), (r.g_cross, r.g_cross_out))[g]
-            for j in range(3):
-                qkv[j] = tot[:, j * wd : (j + 1) * wd]
+            for at, j in enumerate((1, 2, 0)):
+                qkv[j] = tot[:, at * wd : (at + 1) * wd]
             out[...] = jnp.swapaxes(tot[:, 3 * wd :], 0, 1)
         else:
             (r.g_up, r.g_down)[g - 3][...] = tot
@@ -425,53 +451,61 @@
             tot = tot + r.ZR[g, d].astype(F32)
         put_grad(g, tot)
 
-    GT = 128
+    GT = 256 if D % 256 == 0 else 128
     NG = D // GT
 
     def gain_col(k, lo):
         return r.gcols[pl.ds(lo, GT), :][:, k : k + 1]
 
-    def add_gain(k, lo, prod, first):
+    def add_gain(k, lo, prod):
         lane = lax.broadcasted_iota(jnp.int32, (GT, 128), 1)
-        col = jnp.sum(prod, -1, keepdims=True)
+        col = jnp.sum(prod, -1, keepdims=True) / gain_col(k, lo)
         rows = pl.ds(lo, GT)
         r.GA[rows] = r.GA[rows] + jnp.where(lane == k, col, 0.0)
 
-    def grads_attn(g, gains, parts):
-        def step(i, _):
-            lo = pl.multiple_of(i * GT, GT)
-            cols = pl.ds(lo, GT)
-            rows = pl.ds(lo, GT)
-            gs = [p(cols) for p in parts]
-            old = r.W[g, rows].astype(F32)
-            full = jnp.concatenate(gs, 1)
-            lane = lax.broadcasted_iota(jnp.int32, (GT, D), 1)
-            prod = full * old
-            scale = jnp.ones((GT, D), F32)
-            at = 0
-            for k, width in gains:
-                sel = (lane >= at) & (lane < at + width)
-                add_gain(k, lo, jnp.where(sel, prod, 0.0), False)
-                scale = jnp.where(sel, gain_col(k, lo), scale)
-                at += width
-            r.W[g, rows] = (full * scale).astype(BF)
-            return 0
-
-        lax.fori_loop(0, NG, step, 0)
-
-    def prep_attn(g, ks):
+    def scale_of(segs, lo):
+        lane = lax.broadcasted_iota(jnp.int32, (GT, D), 1)
+        scale, end = jnp.ones((GT, D), F32), sum(width for _, width in segs)
+        for k, width in reversed(segs):
+            scale = jnp.where(lane < end, gain_col(k, lo), scale)
+            end -= width
+        return scale
+
+    def prep_attn(g, segs):
         def step(i, _):
             lo = pl.multiple_of(i * GT, GT)
             rows = pl.ds(lo, GT)
             w = r.W[g, rows].astype(F32)
-            for j in range(4):
-                part = w[:, j * wd : (j + 1) * wd]
-                if ks[j] is not None:
-                    part = part * gain_col(ks[j], lo)
-                r.PW[g, j, rows] = part.astype(BF)
+            r.PWO[g, rows] = w[:, 3 * wd :].astype(BF)
+            r.W[g, rows] = (w * scale_of(segs, lo)).astype(BF)
             return 0
 
         lax.fori_loop(0, NG, step, 0)
+
+    def grads_attn(g, segs, parts):
+        def step(i, _):
+            lo = pl.multiple_of(i * GT, GT)
+            cols = rows = pl.ds(lo, GT)
+            full = jnp.concatenate([p(cols) for p in parts], 1)
+            prod = full * r.W[g, rows].astype(F32)
+            at = 0
+            for k, width in segs:
+                lane = lax.broadcasted_iota(jnp.int32, (GT, D), 1)
+                sel = (lane >= at) & (lane < at + width)
+                add_gain(k, lo, jnp.where(sel, prod, 0.0))
+                at += width
+            r.W[g, rows] = (full * scale_of(segs, lo)).astype(BF)
+            return 0
+
+        lax.fori_loop(0, NG, step, 0)
+
+    SEGS = (((0, 3 * wd),), ((1, 3 * wd),), ((3, 2 * wd), (2, wd)))
+
+    def img(ref, cols):
+        return ref[:, :, cols].reshape(IP, GT)
+
+    def txt(ref, cols):
+        return ref[:, :, cols].reshape(TP, GT)
 
     for cp in first:
         cp.wait()
@@ -486,11 +520,24 @@
         r.RS1[rows] = rstd
         r.X1[0, rows] = xh.astype(BF)
         ag1.append(ag_send(r.X1, lo, n))
+    if fused:
+        w_pack(1)
+        w_pack(2)
+    w_send_z(1)
+    w_send_x(1)
+    w_send_z(2)
+    w_send_x(2)
     xh, rstd = ln_fwd(r.text[...])
     r.XHA[...] = xh
     r.RSA[...] = rstd
     r.X1T[0] = xh.astype(BF)
     tag1 = tag(r.X1T)
+    if fused:
+        w_pack(3)
+        w_pack(4)
+    w_send_z(3)
+    w_send_z(4)
+    w_relay(0, (1,))
     prep_valid()
     prep_gains()
     r.GA[...] = jnp.zeros_like(r.GA)
@@ -498,11 +545,23 @@
         rows = pl.ds(lo, n)
         r.DY[0, rows] = (r.GM[rows] * r.valid_i[rows]).astype(BF)
     r.DYT[0] = (r.tcot[...] * r.valid_t[...]).astype(BF)
-    if fused:
-        for g in range(1, 5):
-            w_pack(g)
-    w_relay(0)
-    w_send(1)
+    w_relay(0, (2,))
+
+    PR = 48
+
+    def perm_rows(t, _):
+        lo = pl.multiple_of(t * PR, PR)
+        w, at = t // (AREA // PR), t % (AREA // PR) * PR
+        hit = window_idx(w, at, PR) == lax.broadcasted_iota(jnp.int32, (PR, IP), 1)
+        r.P[pl.ds(lo, PR)] = jnp.where(hit, 1.0, 0.0).astype(BF)
+        return 0
+
+    NP = COUNT * AREA // PR
+    lax.fori_loop(0, NP // 2, perm_rows, 0)
+    w_relay(0, (3,))
+    w_send_x(3)
+    w_send_x(4)
+    lax.fori_loop(NP // 2, NP, perm_rows, 0)
     rel1 = ag_relay(r.X1, ag1)
     agdy = [ag_send(r.DY, lo, n) for lo, n in CH]
     tagdy = tag(r.DYT)
@@ -510,51 +569,30 @@
         for cp in local:
             cp.wait()
     w_ready(0)
-    prep_attn(0, (0, 0, 0, None))
-    w_relay(1)
-    w_send(2)
-
-    def qkv_slot(s):
-        def step(j, _):
-            v = nn(r.X1[s], r.PW[0, j]) * jnp.where(j == 0, SCALE, 1.0)
-            r.QR[j, pl.ds(s * IR, IR)] = v.astype(BF)
-            return 0
-
-        lax.fori_loop(0, 3, step, 0)
-
-    qkv_slot(0)
-    wait_all([a[1] for a in ag1])
-    qkv_slot(1)
-    qkv_slot(2)
-    wait_all(rel1)
-    qkv_slot(3)
-    reldy = ag_relay(r.DY, agdy)
-
+    prep_attn(0, SEGS[0])
+    wait_all([a[1] for a in ag1] + rel1)
+
+    def q_scale(v, at):
+        lane = lax.broadcasted_iota(jnp.int32, (1, v.shape[1]), 1)
+        return (v * jnp.where(lane >= at, SCALE, 1.0)).astype(BF)
+
+    def qkv_slot(i, _):
+        r.QR[pl.ds(pl.multiple_of(i * 2 * IR, 2 * IR), 2 * IR)] = q_scale(
+            nn(r.X1[pl.ds(i * 2, 2)].reshape(2 * IR, D), r.W[0, :, KVQ]), 2 * wd
+        )
+        return 0
+
+    lax.fori_loop(0, 2, qkv_slot, 0)
+    w_relay(1, (1,))
     WG = 3 * AREA
 
-    def perm_chunk(i):
-        n = 16
-
-        def build(t, _):
-            lo = pl.multiple_of(t * n, n)
-            w, a = i * 3 + t // (AREA // n), t % (AREA // n) * n
-            hit = window_idx(w, a, n) == lax.broadcasted_iota(jnp.int32, (n, IP), 1)
-            r.PB[pl.ds(lo, n)] = jnp.where(hit, 1.0, 0.0).astype(BF)
-            return 0
-
-        lax.fori_loop(0, WG // n, build, 0)
-        return pl.ds(pl.multiple_of(i * WG, WG), WG)
-
     def perm_q(i, _):
-        dst = perm_chunk(i)
-
-        def step(j, _):
-            r.QW[j, dst] = nn(r.PB[...], r.QR[j]).astype(BF)
-            return 0
-
-        return lax.fori_loop(0, 3, step, 0)
-
-    lax.fori_loop(0, 3, perm_q, 0)
+        at = pl.ds(pl.multiple_of(i * WG, WG), WG)
+        r.QW[at] = nn(r.P[at], r.QR[...]).astype(BF)
+        return 0
+
+    lax.fori_loop(0, COUNT * AREA // WG, perm_q, 0)
+    w_relay(1, (2,))
 
     def win_fwd(w, _):
         at = pl.ds(pl.multiple_of(w * AREA, AREA), AREA)
@@ -562,70 +600,41 @@
         i1 = lax.broadcasted_iota(jnp.int32, (AREA, AREA), 1)
         good = counts(*window_rows(w, lax.broadcasted_iota(jnp.int32, (1, AREA), 1)))
         ok = jnp.where(i0 == i1, 1.0, jnp.where(good, 1.0, 0.0))
-        ok = jnp.concatenate([ok] * len(masks), 0) > 0.0
-        o, p = attend(r.QW[0, at], r.QW[1, at], r.QW[2, at], ok, masks)
+        ok = jnp.concatenate([ok] * NH, 0) > 0.0
+        o, p = heads.attend(r.QW[at, K], r.QW[at, KV], r.QW[at, Q], ok)
         r.AW[at] = o
         r.PWIN[w] = p
         return 0
 
-    lax.fori_loop(0, COUNT, win_fwd, 0)
+    lax.fori_loop(0, COUNT, win_fwd, 0, unroll=UNROLL)
+    w_relay(1, (3,))
+    MC = [(lo, min(384, IP - lo)) for lo in range(0, IP, 384)]
+    for lo, n in MC:
+        r.AR[lo : lo + n] = tn(r.P[:, lo : lo + n], r.AW[...]).astype(BF)
+
+    def win_out(s, cols):
+        return nt(r.AR[s * IR : (s + 1) * IR], r.PWO[0, cols])
+
+    st1 = rs_far(0, win_out)
+    rs_over(st1)
+    rs_near(st1, win_out)
+
     w_ready(1)
-    w_relay(2)
-    w_send(3)
-    prep_attn(1, (1, 1, 1, None))
-
-    def inv_chunk(s):
-        n = 16
-
-        def build(t, _):
-            lo = pl.multiple_of(t * n, n)
-            k = lax.broadcasted_iota(jnp.int32, (n, 1), 0) + lo
-            hit = slot_inv(s, k) == lax.broadcasted_iota(jnp.int32, (n, COUNT * AREA), 1)
-            r.PTB[pl.ds(lo, n)] = jnp.where(hit, 1.0, 0.0).astype(BF)
-            return 0
-
-        lax.fori_loop(0, IR // n, build, 0)
-
-    def attn_rows(s, _):
-        inv_chunk(s)
-        r.AR[s] = nn(r.PTB[...], r.AW[...]).astype(BF)
-        return 0
-
-    lax.fori_loop(0, 4, attn_rows, 0)
-
-    def wtile(g, j, cols):
-        return r.PW[g, j, cols]
-
-    rs1 = rs_start(0, lambda s, t, cols: nt(r.AR[s], wtile(0, 3, cols)))
-    next(rs1)
-    next(rs1)
-
+    prep_attn(1, SEGS[1])
     wait_all(tag1)
-    xt = r.X1T[...].reshape(TP, D)
-    r.TQ[0] = (nn(xt, r.PW[1, 0]) * SCALE).astype(BF)
-    r.TQ[1] = nn(xt, r.PW[1, 1]).astype(BF)
-    r.TQ[2] = nn(xt, r.PW[1, 2]).astype(BF)
-    ok_t = jnp.concatenate([jnp.where(text_mask(), 1.0, 0.0)] * len(masks), 0) > 0.0
-    o, p = attend(r.TQ[0], r.TQ[1], r.TQ[2], ok_t, masks)
+    r.TQ[...] = q_scale(nn(r.X1T[...].reshape(TP, D), r.W[1, :, KVQ]), 2 * wd)
+    ok_t = jnp.concatenate([jnp.where(text_mask(), 1.0, 0.0)] * NH, 0) > 0.0
+    o, p = heads.attend(r.TQ[:, K], r.TQ[:, KV], r.TQ[:, Q], ok_t)
     r.TA[...] = o
     r.TPR[...] = p
-    trs1 = trs_send(0, nt(r.TA[...], r.PW[1, 3]))
-    next(rs1)
-    st1 = next(rs1)
-    w_ready(2)
-    w_relay(3)
-    w_send(4)
-    prep_attn(2, (2, 3, 3, None))
-
-    tmid = r.text[...] + r.valid_t[...] * trs_sum(0, trs1)
-    r.TMID[...] = tmid
-    xh, rstd = ln_fwd(tmid)
-    r.XHQ[...] = xh
-    r.RSQ[...] = rstd
-    r.X2T[0] = xh.astype(BF)
-    tag2 = tag(r.X2T)
+    trs1 = trs_send(0, nt(r.TA[...], r.PWO[1]))
+    w_relay(2, (1, 2))
+    reldy = ag_relay(r.DY, agdy)
+
     ag2 = []
-    for i, (lo, n) in enumerate(CH):
+
+    def mid_chunk(i):
+        lo, n = CH[i]
         rows = pl.ds(lo, n)
         mid = r.MID[rows] + r.valid_i[rows] * rs_sum(st1, i)
         r.MID[rows] = mid
@@ -634,21 +643,52 @@
         r.RS2[rows] = rstd
         r.X2[0, rows] = xh.astype(BF)
         ag2.append(ag_send(r.X2, lo, n))
+
+    for i in range(len(CH) - 1):
+        mid_chunk(i)
+    w_relay(2, (3,))
+    tmid = r.text[...] + r.valid_t[...] * trs_sum(0, trs1)
+    r.TMID[...] = tmid
+    xh, rstd = ln_fwd(tmid)
+    r.XHQ[...] = xh
+    r.RSQ[...] = rstd
+    r.X2T[0] = xh.astype(BF)
+    tag2 = tag(r.X2T)
+    mid_chunk(len(CH) - 1)
     wait_all([a[1] for a in agdy] + reldy + tagdy)
     sent([a[1] for a in agdy] + [a[0] for a in agdy] + reldy)
 
-    def kv_slot(s):
-        def step(j, _):
-            r.KV[j, pl.ds(s * IR, IR)] = nn(r.X2[s], r.PW[2, j + 1]).astype(BF)
-            return 0
-
-        lax.fori_loop(0, 2, step, 0)
-
-    kv_slot(0)
+    w_ready(2)
+    prep_attn(2, SEGS[2])
+    w_relay(3)
+    rel2 = ag_relay(r.X2, ag2)
     wait_all(tag2)
-    r.CQ[...] = (nn(r.X2T[...].reshape(TP, D), r.PW[2, 0]) * SCALE).astype(BF)
+    r.CQ[...] = (nn(r.X2T[...].reshape(TP, D), r.W[2, :, Q]) * SCALE).astype(BF)
+    wait_all([a[1] for a in ag2] + rel2)
+
+    def kv_slot(i, _):
+        r.KVR[pl.ds(pl.multiple_of(i * 2 * IR, 2 * IR), 2 * IR)] = nn(
+            r.X2[pl.ds(i * 2, 2)].reshape(2 * IR, D), r.W[2, :, KV]
+        ).astype(BF)
+        return 0
+
+    lax.fori_loop(0, 2, kv_slot, 0)
+    HR = NH * TP
+
+    def head(h, width, at):
+        lane = lax.broadcasted_iota(jnp.int32, (1, width), 1)
+        return (lane >= at + h * HD) & (lane < at + (h + 1) * HD)
+
+    def cross_head(h, _):
+        rows = pl.ds(pl.multiple_of(h * TP, TP), TP)
+        qm = jnp.where(head(h, wd, 0), r.CQ[...].astype(F32), 0.0).astype(BF)
+        r.CPD[rows] = softmax(jnp.where(r.cvalid[...] > 0.0, nt(qm, r.KVR[:, K]), NEG))
+        return 0
+
+    lax.fori_loop(0, NH, cross_head, 0)
+    r.CA[...] = heads.values(r.CPD[0:HR], r.KVR[...])
+    trs2 = trs_send(1, nt(r.CA[...], r.PWO[2]))
     w_ready(3)
-    w_relay(4)
 
     def prep_up(i, _):
         lo = pl.multiple_of(i * GT, GT)
@@ -657,55 +697,28 @@
         return 0
 
     lax.fori_loop(0, NG, prep_up, 0)
-    wait_all([a[1] for a in ag2])
-    kv_slot(1)
-    rel2 = ag_relay(r.X2, ag2)
-    kv_slot(2)
-    wait_all(rel2)
-    kv_slot(3)
-
-    def head(h):
-        lane = lax.broadcasted_iota(jnp.int32, (1, wd), 1)
-        return jnp.where((lane >= h * HD) & (lane < (h + 1) * HD), 1.0, 0.0).astype(BF)
-
-    def cross_head(h, _):
-        rows = pl.ds(pl.multiple_of(h * TP, TP), TP)
-        qm = r.CQ[...] * head(h)
-        s = jnp.where(r.cvalid[...] > 0.0, nt(qm, r.KV[0]), NEG)
-        e = jnp.exp(s - jnp.max(s, -1, keepdims=True))
-        r.CP[rows] = (e * (1.0 / jnp.sum(e, -1, keepdims=True))).astype(BF)
-        return 0
-
-    lax.fori_loop(0, len(masks), cross_head, 0)
-    r.CA[...] = merge_heads(nn(r.CP[...], r.KV[1]), masks).astype(BF)
-    trs2 = trs_send(1, nt(r.CA[...], r.PW[2, 3]))
-    w_ready(4)
-
-    def mlp_tile(xb, dyb, cols):
+    w_relay(4, (1,))
+
+    HT = 256 if hid % 256 == 0 else hid
+    NHT = hid // HT
+
+    def up_tile(xb, cols):
         u = nn(xb, r.W[3, :, cols])
-        th = jnp.tanh(GELU_C * (u + GELU_A * u * u * u))
-        act = 0.5 * u * (1.0 + th)
-        slope = 0.5 * (1.0 + th) + 0.5 * u * (1.0 - th * th) * (
-            GELU_C * (1.0 + 3.0 * GELU_A * u * u)
-        )
-        ga = nn(dyb, r.W[4, :, cols])
-        return act.astype(BF), (ga * slope).astype(BF)
-
-    HT = 256 if hid % 256 == 0 else hid
-
-    def mlp_slot(s):
+        u2 = u * u
+        th = jnp.tanh(u * (GELU_C + GELU_C * GELU_A * u2))
+        half = 0.5 + 0.5 * th
+        slope = half + (u * (1.0 - th * th)) * (0.5 * GELU_C + 1.5 * GELU_C * GELU_A * u2)
+        return (u * half).astype(BF), slope.astype(BF)
+
+    def up_slot(s):
         def step(t, _):
             cols = pl.ds(pl.multiple_of(t * HT, HT), HT)
-            a, gu = mlp_tile(r.X2[s], r.DY[s], cols)
-            r.ACT[s, :, cols] = a
-            r.GU[s, :, cols] = gu
+            r.ACT[s, :, cols], r.GU[s, :, cols] = up_tile(r.X2[s], cols)
             return 0
 
-        lax.fori_loop(0, hid // HT, step, 0)
-
-    rs2 = rs_start(1, lambda s, t, cols: nt(r.ACT[s], r.W[4, cols]))
-    mlp_slot(3)
-    next(rs2)
+        lax.fori_loop(0, NHT, step, 0)
+
+    up_slot(0)
     tlate = r.TMID[...] + r.valid_t[...] * trs_sum(1, trs2)
     r.TMID[...] = tlate
     xh, rstd = ln_fwd(tlate)
@@ -713,210 +726,192 @@
     r.RSL[...] = rstd
     r.XT[0] = xh.astype(BF)
     tag3 = tag(r.XT)
-    mlp_slot(2)
-    next(rs2)
+    w_relay(4, (2,))
+    up_slot(1)
+    up_slot(2)
+    w_relay(4, (3,))
+    up_slot(3)
     wait_all(tag3)
 
-    def mlp_text(t, _):
+    def up_text(t, _):
         cols = pl.ds(pl.multiple_of(t * HT, HT), HT)
-        a, gu = mlp_tile(r.XT[...].reshape(TP, D), r.DYT[...].reshape(TP, D), cols)
-        r.ACTT[:, cols] = a
-        r.GUT[:, cols] = gu
-        return 0
-
-    lax.fori_loop(0, hid // HT, mlp_text, 0)
+        r.ACTT[:, cols], r.GUT[:, cols] = up_tile(r.XT[...].reshape(TP, D), cols)
+        return 0
+
+    lax.fori_loop(0, NHT, up_text, 0)
+    w_ready(4)
+
+    def back_text(t, _):
+        cols = pl.ds(pl.multiple_of(t * HT, HT), HT)
+        ga = nn(r.DYT[...].reshape(TP, D), r.W[4, :, cols])
+        r.GUT[:, cols] = (ga * r.GUT[:, cols].astype(F32)).astype(BF)
+        return 0
+
+    lax.fori_loop(0, NHT, back_text, 0)
     trs4 = trs_send(3, nt(r.GUT[...], r.W[3]))
     trs3 = trs_send(2, nt(r.ACTT[...], r.W[4]))
-    mlp_slot(1)
-    next(rs2)
+
+    def back_slot(i, _):
+        s, t = i // NHT, i % NHT
+        cols = pl.ds(pl.multiple_of(t * HT, HT), HT)
+        ga = nn(r.DY[s], r.W[4, :, cols])
+        r.GU[s, :, cols] = (ga * r.GU[s, :, cols].astype(F32)).astype(BF)
+        return 0
+
+    lax.fori_loop(0, 4 * NHT, back_slot, 0)
     gtl = r.tcot[...] + ln_bwd(trs_sum(3, trs4), r.XHL[...], r.RSL[...])
     r.GTX[...] = gtl
     r.DC[0] = (gtl * r.valid_t[...]).astype(BF)
     tag4 = tag(r.DC)
-    mlp_slot(0)
-    st2 = next(rs2)
-
-    wait_all(tag4)
-    da = nn(r.DC[...].reshape(TP, D), r.PW[2, 3]).astype(BF)
-    das = stack_heads(da, masks)
-    r.CDA[...] = da
-
-    def cross_head_back(h, _):
-        rows = pl.ds(pl.multiple_of(h * TP, TP), TP)
-        dp = nt(r.CDA[...] * head(h), r.KV[1])
-        pf = r.CP[rows].astype(F32)
-        pd = pf * dp
-        r.PB[rows] = (pd - pf * jnp.sum(pd, -1, keepdims=True)).astype(BF)
-        return 0
-
-    lax.fori_loop(0, len(masks), cross_head_back, 0)
-    HR = len(masks) * TP
-    ds = r.PB[0:HR]
-    r.CDQ[...] = (merge_heads(nn(ds, r.KV[0]), masks) * SCALE).astype(BF)
-    r.DKV[0] = tn(ds, stack_heads(r.CQ[...], masks)).astype(BF)
-    r.DKV[1] = tn(r.CP[...], das).astype(BF)
-    trs5 = trs_send(4, nt(r.CDQ[...], r.PW[2, 0]))
+
+    def down_out(s, cols):
+        return nt(r.ACT[s], r.W[4, cols])
+
+    st2 = rs_far(1, down_out)
+    rs_near(st2, down_out)
 
     def gd_step(i, _):
         lo = pl.multiple_of(i * GT, GT)
         cols = pl.ds(lo, GT)
-        full = tn(r.DY[:, :, cols].reshape(IP, GT), r.ACT[...].reshape(IP, hid))
-        full = full + tn(r.DYT[:, :, cols].reshape(TP, GT), r.ACTT[...])
-        r.W[4, pl.ds(lo, GT)] = full.astype(BF)
+        full = tn(img(r.DY, cols), r.ACT[...].reshape(IP, hid)) + tn(txt(r.DYT, cols), r.ACTT[...])
+        r.W[4, cols] = full.astype(BF)
         return 0
 
     lax.fori_loop(0, NG, gd_step, 0)
     g_start(4)
 
-    def mid_partial(s, t, cols):
-        at = pl.ds(s * IR, IR)
-        return (
-            nt(r.GU[s], r.W[3, cols])
-            + nt(r.DKV[0, at], wtile(2, 1, cols))
-            + nt(r.DKV[1, at], wtile(2, 2, cols))
-        )
-
-    rs3 = rs_start(0, mid_partial)
-    for _ in range(4):
-        st3 = next(rs3)
+    wait_all(tag4)
+    da = nn(r.DC[...].reshape(TP, D), r.PWO[2]).astype(BF)
+    das = heads.place_second(da)
+    r.CDA[...] = da
+
+    def cross_head_back(h, _):
+        rows = pl.ds(pl.multiple_of(h * TP, TP), TP)
+        dah = r.CDA[...].astype(F32)
+        dah = jnp.concatenate([jnp.zeros_like(dah), dah], 1)
+        dah = jnp.where(head(h, 2 * wd, wd), dah, 0.0).astype(BF)
+        ds = score_back(r.CPD[rows], nt(dah, r.KVR[...]))
+        r.CPD[pl.ds(pl.multiple_of(HR + h * TP, TP), TP)] = ds
+        return 0
+
+    lax.fori_loop(0, NH, cross_head_back, 0)
+    r.CDQ[...] = (merge_heads(nn(r.CPD[HR : 2 * HR], r.KVR[:, K]), heads.own) * SCALE).astype(BF)
+    trs5 = trs_send(4, nt(r.CDQ[...], r.W[2, :, Q]))
+    both = jnp.concatenate([das, heads.place_first(r.CQ[...])], 0)
+    for lo, n in MC:
+        r.DKV[lo : lo + n] = tn(r.CPD[:, lo : lo + n], both).astype(BF)
+
+    def mid_partial(s, cols):
+        return nt(r.GU[s], r.W[3, cols]) + nt(r.DKV[s * IR : (s + 1) * IR], r.W[2, cols, KV])
+
+    st3 = rs_far(0, mid_partial)
+    rs_over(st3)
+    rs_near(st3, mid_partial)
 
     def gu_step(i, _):
         lo = pl.multiple_of(i * GT, GT)
         cols = pl.ds(lo, GT)
-        rows = pl.ds(lo, GT)
-        full = tn(r.X2[:, :, cols].reshape(IP, GT), r.GU[...].reshape(IP, hid))
-        full = full + tn(r.XT[:, :, cols].reshape(TP, GT), r.GUT[...])
-        add_gain(4, lo, full * r.W[3, rows].astype(F32) * (1.0 / gain_col(4, lo)), False)
-        r.W[3, rows] = (full * gain_col(4, lo)).astype(BF)
+        full = tn(img(r.X2, cols), r.GU[...].reshape(IP, hid)) + tn(txt(r.XT, cols), r.GUT[...])
+        add_gain(4, lo, full * r.W[3, cols].astype(F32))
+        r.W[3, cols] = (full * gain_col(4, lo)).astype(BF)
         return 0
 
     lax.fori_loop(0, NG, gu_step, 0)
     g_start(3)
-
-    gtm = r.GTX[...] + ln_bwd(trs_sum(4, trs5), r.XHQ[...], r.RSQ[...])
-    r.GTX[...] = gtm
-    r.DWT[0] = (gtm * r.valid_t[...]).astype(BF)
-    tag5 = tag(r.DWT)
-
-    for i in range(len(CH)):
+    g_mid(4)
+
+    ag3 = []
+
+    def grad_chunk(i):
         lo, n = CH[i]
-        rows = pl.ds(lo, n)
-        r.MID[rows] = r.MID[rows] + r.valid_i[rows] * rs_sum(st2, i)
-    out_i = rows_out(0, r.MID, r.image_out)
-    r.text_out[0] = r.TMID[...] + r.valid_t[...] * trs_sum(2, trs3)
-
-    ag3 = []
-    for i, (lo, n) in enumerate(CH):
         rows = pl.ds(lo, n)
         gm = r.GM[rows] + ln_bwd(rs_sum(st3, i), r.XH2[rows], r.RS2[rows])
         r.GM[rows] = gm
         r.DY[0, rows] = (gm * r.valid_i[rows]).astype(BF)
         ag3.append(ag_send(r.DY, lo, n))
 
+    for i in range(len(CH) - 1):
+        grad_chunk(i)
+    gtm = r.GTX[...] + ln_bwd(trs_sum(4, trs5), r.XHQ[...], r.RSQ[...])
+    r.GTX[...] = gtm
+    r.DWT[0] = (gtm * r.valid_t[...]).astype(BF)
+    tag5 = tag(r.DWT)
+    grad_chunk(len(CH) - 1)
+    rs_over(st2)
+    r.text_out[0] = r.TMID[...] + r.valid_t[...] * trs_sum(2, trs3)
+
     grads_attn(
         2,
-        ((2, wd), (3, 2 * wd)),
+        SEGS[2],
         (
-            lambda cols: tn(r.X2T[:, :, cols].reshape(TP, GT), r.CDQ[...]),
-            lambda cols: tn(r.X2[:, :, cols].reshape(IP, GT), r.DKV[0]),
-            lambda cols: tn(r.X2[:, :, cols].reshape(IP, GT), r.DKV[1]),
-            lambda cols: tn(r.DC[:, :, cols].reshape(TP, GT), r.CA[...]),
+            lambda cols: tn(img(r.X2, cols), r.DKV[...]),
+            lambda cols: tn(txt(r.X2T, cols), r.CDQ[...]),
+            lambda cols: tn(txt(r.DC, cols), r.CA[...]),
         ),
     )
     g_start(2)
-    g_mid(4)
 
     wait_all(tag5)
-    da = nn(r.DWT[...].reshape(TP, D), r.PW[1, 3]).astype(BF)
-    dq, dk, dv = attend_back(r.TQ[0], r.TQ[1], r.TQ[2], r.TPR[...], da, masks)
-    r.DTQ[0] = dq
-    r.DTQ[1] = dk
-    r.DTQ[2] = dv
-    trs6 = trs_send(
-        5,
-        nt(r.DTQ[0], r.PW[1, 0]) + nt(r.DTQ[1], r.PW[1, 1]) + nt(r.DTQ[2], r.PW[1, 2]),
-    )
-    rel3 = ag_relay(r.DY, ag3)
-
-    def da_slot(s):
-        r.DKV[0, pl.ds(s * IR, IR)] = nn(r.DY[s], r.PW[0, 3]).astype(BF)
-
-    da_slot(0)
-    wait_all([a[1] for a in ag3])
-    da_slot(1)
-    da_slot(2)
+    da = nn(r.DWT[...].reshape(TP, D), r.PWO[1]).astype(BF)
+    dkv, dq = heads.attend_back(r.TQ[:, K], r.TQ[:, KV], r.TQ[:, Q], r.TPR[...], da)
+    r.DTQ[:, KV] = dkv
+    r.DTQ[:, Q] = dq
+    trs6 = trs_send(5, nt(r.DTQ[...], r.W[1, :, KVQ]))
     grads_attn(
         1,
-        ((1, 3 * wd),),
-        tuple(
-            (lambda cols, j=j: tn(r.X1T[:, :, cols].reshape(TP, GT), r.DTQ[j]))
-            for j in range(3)
-        )
-        + (lambda cols: tn(r.DWT[:, :, cols].reshape(TP, GT), r.TA[...]),),
+        SEGS[1],
+        (
+            lambda cols: tn(txt(r.X1T, cols), r.DTQ[...]),
+            lambda cols: tn(txt(r.DWT, cols), r.TA[...]),
+        ),
     )
     g_start(1)
+    rel3 = ag_relay(r.DY, ag3)
+    wait_all([a[1] for a in ag3] + rel3)
+
+    def da_slot(i, _):
+        r.DA[pl.ds(pl.multiple_of(i * 2 * IR, 2 * IR), 2 * IR)] = nn(
+            r.DY[pl.ds(i * 2, 2)].reshape(2 * IR, D), r.PWO[0]
+        ).astype(BF)
+        return 0
+
+    lax.fori_loop(0, 2, da_slot, 0)
+
+    def perm_d(i, _):
+        at = pl.ds(pl.multiple_of(i * WG, WG), WG)
+        r.AW[at] = nn(r.P[at], r.DA[...]).astype(BF)
+        return 0
+
+    lax.fori_loop(0, COUNT * AREA // WG, perm_d, 0)
     g_mid(3)
-    wait_all(rel3)
-    da_slot(3)
-
-    def perm_d(i, _):
-        dst = perm_chunk(i)
-        r.AW[dst] = nn(r.PB[...], r.DKV[0]).astype(BF)
-        return 0
-
-    lax.fori_loop(0, 3, perm_d, 0)
 
     def win_bwd(w, _):
         at = pl.ds(pl.multiple_of(w * AREA, AREA), AREA)
-        dq, dk, dv = attend_back(
-            r.QW[0, at], r.QW[1, at], r.QW[2, at], r.PWIN[w], r.AW[at], masks
-        )
-        r.QW[0, at] = dq
-        r.QW[1, at] = dk
-        r.QW[2, at] = dv
-        return 0
-
-    lax.fori_loop(0, COUNT, win_bwd, 0)
+        dkv, dq = heads.attend_back(r.QW[at, K], r.QW[at, KV], r.QW[at, Q], r.PWIN[w], r.AW[at])
+        r.QW[at, KV] = dkv
+        r.QW[at, Q] = dq
+        return 0
+
+    lax.fori_loop(0, COUNT, win_bwd, 0, unroll=UNROLL)
     g_mid(2)
-
-    def back_rows(s):
-        inv_chunk(s)
-
-        def step(j, _):
-            r.QR[j, pl.ds(s * IR, IR)] = nn(r.PTB[...], r.QW[j]).astype(BF)
-            return 0
-
-        lax.fori_loop(0, 3, step, 0)
-
-    def win_partial(s, t, cols):
-        at = pl.ds(s * IR, IR)
-        return (
-            nt(r.QR[0, at], wtile(0, 0, cols))
-            + nt(r.QR[1, at], wtile(0, 1, cols))
-            + nt(r.QR[2, at], wtile(0, 2, cols))
-        )
-
-    rs4 = rs_start(1, win_partial)
-    back_rows(3)
-    next(rs4)
-    back_rows(2)
-    next(rs4)
-    back_rows(1)
-    back_rows(0)
+    for lo, n in MC:
+        r.QR[lo : lo + n] = tn(r.P[:, lo : lo + n], r.QW[...]).astype(BF)
+
+    def win_partial(s, cols):
+        return nt(r.QR[s * IR : (s + 1) * IR], r.W[0, cols, KVQ])
+
+    st4 = rs_far(0, win_partial)
+    rs_over(st4)
+    rs_near(st4, win_partial)
     grads_attn(
         0,
-        ((0, 3 * wd),),
-        tuple(
-            (lambda cols, j=j: tn(r.X1[:, :, cols].reshape(IP, GT), r.QR[j]))
-            for j in range(3)
-        )
-        + (
-            lambda cols: tn(r.DY[:, :, cols].reshape(IP, GT), r.AR[...].reshape(IP, wd)),
+        SEGS[0],
+        (
+            lambda cols: tn(img(r.X1, cols), r.QR[...]),
+            lambda cols: tn(img(r.DY, cols), r.AR[...]),
         ),
     )
     g_start(0)
-    next(rs4)
-    st4 = next(rs4)
     g_mid(1)
 
     r.GB[0] = jnp.swapaxes(r.GA[...], 0, 1)[0:8]
@@ -925,11 +920,17 @@
     gc.wait_recv()
     r.GB[1] = r.GB[0] + r.GR[0]
     gc = push(r.GB.at[1], r.GR.at[1], yp)
+    for i in range(len(CH)):
+        lo, n = CH[i]
+        rows = pl.ds(lo, n)
+        r.MID[rows] = r.MID[rows] + r.valid_i[rows] * rs_sum(st2, i)
+    out_i = rows_out(0, r.MID, r.image_out)
     g_fin(4)
     gc.wait_recv()
     if fused:
         r.GB[2] = r.GB[1] + r.GR[1]
         gc = push(r.GB.at[2], r.GR.at[2], xpeer)
+        g_fin(3)
         g_mid(0)
         gc.wait_recv()
         r.GZ[z] = r.GB[2] + r.GR[2]
@@ -940,7 +941,6 @@
         rows = pl.ds(lo, n)
         r.GM[rows] = r.GM[rows] + ln_bwd(rs_sum(st4, i), r.XH1[rows], r.RS1[rows])
     out_g = rows_out(1, r.GM, r.image_grad)
-    g_fin(3)
     g_fin(2)
     g_fin(1)
     if fused:
@@ -995,7 +995,6 @@
     V = pltpu.VMEM
     scratch = {
         "W": V((5, D, D), BF),
-        "PW": V((3, 4, D, wd), BF),
         "X1": V((4, IR, D), BF),
         "X2": V((4, IR, D), BF),
         "DY": V((4, IR, D), BF),
@@ -1019,28 +1018,29 @@
         "RSA": V((TR, 1), F32),
         "RSQ": V((TR, 1), F32),
         "RSL": V((TR, 1), F32),
-        "QR": V((3, IP, wd), BF),
-        "QW": V((3, ROWS, wd), BF),
+        "PWO": V((3, D, wd), BF),
+        "P": V((ROWS, IP), BF),
+        "QR": V((IP, 3 * wd), BF),
+        "QW": V((ROWS, 3 * wd), BF),
+        "AW": V((ROWS, wd), BF),
+        "AR": V((IP, wd), BF),
+        "DA": V((IP, wd), BF),
+        "KVR": V((IP, 2 * wd), BF),
+        "DKV": V((IP, 2 * wd), BF),
+        "CPD": V((2 * NH * TP, IP), BF),
+        "TQ": V((TP, 3 * wd), BF),
+        "DTQ": V((TP, 3 * wd), BF),
+        "CDA": V((TP, wd), BF),
         "PWIN": V((COUNT, NH * AREA, AREA), BF),
-        "AW": V((ROWS, wd), BF),
-        "AR": V((4, IR, wd), BF),
-        "KV": V((2, IP, wd), BF),
-        "DKV": V((2, IP, wd), BF),
         "CQ": V((TP, wd), BF),
         "CDQ": V((TP, wd), BF),
-        "CDA": V((TP, wd), BF),
         "CA": V((TP, wd), BF),
-        "CP": V((NH * TP, IP), BF),
-        "TQ": V((3, TP, wd), BF),
-        "DTQ": V((3, TP, wd), BF),
         "TA": V((TP, wd), BF),
         "TPR": V((NH * TP, TP), BF),
         "ACT": V((4, IR, hid), BF),
         "GU": V((4, IR, hid), BF),
         "ACTT": V((TP, hid), BF),
         "GUT": V((TP, hid), BF),
-        "PB": V((3 * AREA, IP), BF),
-        "PTB": V((IR, ROWS), BF),
         "RB": V((2, 5, IR, D), BF),
         "OB": V((2, IR, D), F32),
         "TS": V((6, 3, TR, D), BF),
@@ -1126,7 +1126,7 @@
     else:
 
         def pack(w, out):
-            return jnp.concatenate([w[0], w[1], w[2], out.T], 1)
+            return jnp.concatenate([w[1], w[2], w[0], out.T], 1)
 
         packed = [
             pack(w_window, w_window_out),
@@ -1147,7 +1147,8 @@
         gains = [lax.psum(g, "seq") for g in gains]
         grads = []
         for g in G[:3]:
-            grads += [g[:, : 3 * wd].reshape(sr, 3, wd).transpose(1, 0, 2), g[:, 3 * wd :].T]
+            qkv = g[:, : 3 * wd].reshape(sr, 3, wd).transpose(1, 0, 2)
+            grads += [jnp.roll(qkv, 1, 0), g[:, 3 * wd :].T]
         grads += [G[3], G[4]]
     image_out, text_out, image_grad, text_grad = rows
     return (

time: 225 us -> 212 us (0.942)
  Pallas kernels: 221 us -> 208 us
    pallas_call x1, Pallas kernels: 218 us -> 205 us  [run_kernel(): pl.pallas_call(functools.partial(kernel, cfg), out_shape=[jax.ShapeDtypeS...]
where the time goes in v1:
time: 212 us; the launch traced here: 210 us
  Pallas kernels  208 us (98%)
    pallas_call x1, Pallas kernels, run_kernel(): pl.pallas_call(functools.partial(kernel, cfg), out_shape=[jax.ShapeDtypeS...  205 us

profile of v1, /device:TPU:9, one launch (start us, length us, event | category | flops | bytes accessed | tf_op | source)
XLA Modules:
  0.0 209.9 jit_solution(10752809792420304309)
XLA Ops:
  1.3 204.9 %shard_map.323 = (f32[324,1,768]{2,1,0:T(1,128)}, f32[1,32,768]{2,1,0:T(8,128)}, f32[324,1,768]{2,1,0:T(1,128)}, f32[1,32,768]{2,1,0:T(8,128)}, f32[3,96,192]{2,...) custom-call(f32[324,1,768]{2,1,0:T(1,128)} %bitcast.8, ...), custom_call_target="tpu_custom_call" | custom-call | tf_op jit(solution)/shard_map/pallas_call | solution.py:1068
  206.2 3.5 %shard_map.324 = (f32[324,1,768]{2,1,0:T(1,128)}, f32[1,32,768]{2,1,0:T(8,128)}, f32[324,1,768]{2,1,0:T(1,128)}, f32[1,32,768]{2,1,0:T(8,128)}, f32[3,96,192]{2,...) custom-call(f32[324,1,768]{2,1,0:T(1,128)} %get-tuple-element.51.ref, ...), custom_call_target="tpu_custom_call" | custom-call | tf_op jit(solution)/shard_map/pallas_call | solution.py:1175

commit v2 on v1

--- a/solution.py
+++ b/solution.py
@@ -146,6 +146,23 @@
     def zpeer(d):
         return {"seq": zid(d) * 2 + x}
 
+    args_in = {
+        n: pltpu.make_async_copy(getattr(r, "h_" + n), getattr(r, n), r.isem.at[i])
+        for i, n in enumerate(cfg.small_in)
+    }
+
+    def need(*names):
+        for n in names:
+            args_in.pop(n).wait()
+
+    results = []
+
+    def emit(*names):
+        for n in names:
+            i = cfg.small_out.index(n)
+            results.append(pltpu.make_async_copy(getattr(r, n), getattr(r, "o_" + n), r.osem.at[i]))
+            results[-1].start()
+
     cut = image_shard // 8 * 8
     whole = pl.ds(0, cut)
     rest = pl.ds(cut, image_shard - cut)
@@ -167,7 +184,7 @@
         return cps
 
     first = rows_in(0, r.image, r.MID) + rows_in(1, r.icot, r.GM)
-    for cp in first:
+    for cp in first + list(args_in.values()):
         cp.start()
 
     barrier = pltpu.get_barrier_semaphore()
@@ -202,6 +219,10 @@
             cp.wait_send()
         pending[:] = [a for a in pending if all(a is not b for b in cps)]
 
+    def wait_all(cps):
+        for cp in cps:
+            cp.wait_recv()
+
     def rows_of(seq_index):
         return pl.ds(pl.multiple_of(seq_index * sr, sr), sr)
 
@@ -220,12 +241,13 @@
                 for d in range(1, nz)
             ]
 
-    def w_relay(g, ds=None):
-        if not fused:
-            return
-        for d in ds or range(1, nz):
-            if d >= nz:
-                continue
+    relays = [(g, d) for g in range(5) for d in range(1, nz)]
+
+    def w_relay(n):
+        for _ in range(n if fused else 0):
+            if not relays:
+                return
+            g, d = relays.pop(0)
             wz[g][d - 1].wait_recv()
             at = rows_of(zback(d) * 2 + x)
             wx[g].append(
@@ -235,8 +257,9 @@
     def w_ready(g):
         if not fused:
             return
-        for cp in wx[g]:
-            cp.wait_recv()
+        while relays and relays[0][0] <= g:
+            w_relay(1)
+        wait_all(wx[g])
         sent(wz[g] + wx[g])
 
     def w_pack(g):
@@ -251,6 +274,7 @@
         r.W[g, rows_of(sq)] = full.astype(BF)
 
     if fused:
+        need("w_window", "w_window_out")
         w_pack(0)
     pl.semaphore_wait(barrier, len(greet))
     w_send_z(0)
@@ -259,6 +283,8 @@
         local = [pltpu.make_async_copy(r.wfull.at[g], r.W.at[g], r.lsem.at[g]) for g in range(5)]
         for cp in local:
             cp.start()
+
+    need("page_dims", "shifts", "text_length")
 
     size_r, size_c = r.page_dims[0, 0], r.page_dims[0, 1]
     shift_r, shift_c = r.shifts[0, 0], r.shifts[0, 1]
@@ -335,10 +361,6 @@
             over.wait_recv()
             out.append(push(X.at[2, pl.ds(lo, n)], X.at[3, pl.ds(lo, n)], core))
         return out
-
-    def wait_all(cps):
-        for cp in cps:
-            cp.wait_recv()
 
     def tag(T):
         return [push(T.at[0], T.at[i + 1], peers[i]) for i in range(3)]
@@ -408,25 +430,30 @@
 
     gx, gzc = {}, {}
 
+    def g_of(g):
+        return {0: r.GWN, 3: r.GUP, 4: r.GDN}.get(g, r.W.at[g])
+
     def g_start(g):
         if not fused:
             return
         gx[g] = [
-            push(r.W.at[g, rows_of(zid(d) * 2 + (1 - x))], r.XR.at[g, d], xpeer)
+            push(g_of(g).at[rows_of(zid(d) * 2 + (1 - x))], r.XR.at[g, d], xpeer)
             for d in [*range(1, nz), 0]
         ]
-
-    def g_mid(g):
+        gzc[g] = []
+        waiting.extend((g, d) for d in range(1, nz))
+
+    waiting = []
+
+    def g_mid(n):
         if not fused:
             return
-        gzc[g] = []
-        for i, d in enumerate([*range(1, nz), 0]):
-            gx[g][i].wait_recv()
-            if d == 0:
-                continue
-            at = rows_of(zid(d) * 2 + x)
-            r.W[g, at] = (r.W[g, at].astype(F32) + r.XR[g, d].astype(F32)).astype(BF)
-            gzc[g].append(push(r.W.at[g, at], r.ZR.at[g, d - 1], zpeer(d)))
+        for _ in range(n):
+            g, d = waiting.pop(0)
+            gx[g][d - 1].wait_recv()
+            at, G = rows_of(zid(d) * 2 + x), g_of(g)
+            G[at] = (G[at].astype(F32) + r.XR[g, d].astype(F32)).astype(BF)
+            gzc[g].append(push(G.at[at], r.ZR.at[g, d - 1], zpeer(d)))
 
     def put_grad(g, tot):
         if g < 3:
@@ -434,19 +461,23 @@
             for at, j in enumerate((1, 2, 0)):
                 qkv[j] = tot[:, at * wd : (at + 1) * wd]
             out[...] = jnp.swapaxes(tot[:, 3 * wd :], 0, 1)
+            name = ("g_window", "g_text", "g_cross")[g]
+            emit(name, name + "_out")
         else:
             (r.g_up, r.g_down)[g - 3][...] = tot
+            emit(("g_up", "g_down")[g - 3])
 
     def put_gains(tot):
         outs = (r.gg_window, r.gg_text, r.gg_cross, r.gg_memory, r.gg_mlp)
         for k, out in enumerate(outs):
             out[...] = tot[k : k + 1].reshape(D)
+        emit("gg_window", "gg_text", "gg_cross", "gg_memory", "gg_mlp")
 
     def g_fin(g):
         if not fused:
             return
-        wait_all(gzc[g])
-        tot = r.W[g, rows_of(sq)].astype(F32) + r.XR[g, 0].astype(F32)
+        wait_all(gzc[g] + gx[g][-1:])
+        tot = g_of(g)[rows_of(sq)].astype(F32) + r.XR[g, 0].astype(F32)
         for d in range(nz - 1):
             tot = tot + r.ZR[g, d].astype(F32)
         put_grad(g, tot)
@@ -494,7 +525,7 @@
                 sel = (lane >= at) & (lane < at + width)
                 add_gain(k, lo, jnp.where(sel, prod, 0.0))
                 at += width
-            r.W[g, rows] = (full * scale_of(segs, lo)).astype(BF)
+            g_of(g)[rows] = (full * scale_of(segs, lo)).astype(BF)
             return 0
 
         lax.fori_loop(0, NG, step, 0)
@@ -521,23 +552,26 @@
         r.X1[0, rows] = xh.astype(BF)
         ag1.append(ag_send(r.X1, lo, n))
     if fused:
+        need("w_text", "w_text_out", "w_cross", "w_cross_out")
         w_pack(1)
         w_pack(2)
     w_send_z(1)
-    w_send_x(1)
     w_send_z(2)
-    w_send_x(2)
+    need("text")
     xh, rstd = ln_fwd(r.text[...])
     r.XHA[...] = xh
     r.RSA[...] = rstd
     r.X1T[0] = xh.astype(BF)
     tag1 = tag(r.X1T)
     if fused:
+        need("w_up", "w_down")
         w_pack(3)
         w_pack(4)
     w_send_z(3)
     w_send_z(4)
-    w_relay(0, (1,))
+    w_relay(1)
+    w_send_x(1)
+    need("tcot", *(n for n in cfg.small_in if n.startswith("gain")))
     prep_valid()
     prep_gains()
     r.GA[...] = jnp.zeros_like(r.GA)
@@ -545,7 +579,7 @@
         rows = pl.ds(lo, n)
         r.DY[0, rows] = (r.GM[rows] * r.valid_i[rows]).astype(BF)
     r.DYT[0] = (r.tcot[...] * r.valid_t[...]).astype(BF)
-    w_relay(0, (2,))
+    w_relay(1)
 
     PR = 48
 
@@ -558,9 +592,8 @@
 
     NP = COUNT * AREA // PR
     lax.fori_loop(0, NP // 2, perm_rows, 0)
-    w_relay(0, (3,))
-    w_send_x(3)
-    w_send_x(4)
+    w_relay(1)
+    w_send_x(2)
     lax.fori_loop(NP // 2, NP, perm_rows, 0)
     rel1 = ag_relay(r.X1, ag1)
     agdy = [ag_send(r.DY, lo, n) for lo, n in CH]
@@ -583,7 +616,8 @@
         return 0
 
     lax.fori_loop(0, 2, qkv_slot, 0)
-    w_relay(1, (1,))
+    w_relay(1)
+    w_send_x(3)
     WG = 3 * AREA
 
     def perm_q(i, _):
@@ -592,7 +626,7 @@
         return 0
 
     lax.fori_loop(0, COUNT * AREA // WG, perm_q, 0)
-    w_relay(1, (2,))
+    w_relay(1)
 
     def win_fwd(w, _):
         at = pl.ds(pl.multiple_of(w * AREA, AREA), AREA)
@@ -607,7 +641,8 @@
         return 0
 
     lax.fori_loop(0, COUNT, win_fwd, 0, unroll=UNROLL)
-    w_relay(1, (3,))
+    w_relay(1)
+    w_send_x(4)
     MC = [(lo, min(384, IP - lo)) for lo in range(0, IP, 384)]
     for lo, n in MC:
         r.AR[lo : lo + n] = tn(r.P[:, lo : lo + n], r.AW[...]).astype(BF)
@@ -628,7 +663,7 @@
     r.TA[...] = o
     r.TPR[...] = p
     trs1 = trs_send(0, nt(r.TA[...], r.PWO[1]))
-    w_relay(2, (1, 2))
+    w_relay(2)
     reldy = ag_relay(r.DY, agdy)
 
     ag2 = []
@@ -646,7 +681,7 @@
 
     for i in range(len(CH) - 1):
         mid_chunk(i)
-    w_relay(2, (3,))
+    w_relay(1)
     tmid = r.text[...] + r.valid_t[...] * trs_sum(0, trs1)
     r.TMID[...] = tmid
     xh, rstd = ln_fwd(tmid)
@@ -660,10 +695,11 @@
 
     w_ready(2)
     prep_attn(2, SEGS[2])
-    w_relay(3)
+    w_relay(2)
     rel2 = ag_relay(r.X2, ag2)
     wait_all(tag2)
     r.CQ[...] = (nn(r.X2T[...].reshape(TP, D), r.W[2, :, Q]) * SCALE).astype(BF)
+    w_relay(1)
     wait_all([a[1] for a in ag2] + rel2)
 
     def kv_slot(i, _):
@@ -673,6 +709,7 @@
         return 0
 
     lax.fori_loop(0, 2, kv_slot, 0)
+    w_relay(1)
     HR = NH * TP
 
     def head(h, width, at):
@@ -688,6 +725,7 @@
     lax.fori_loop(0, NH, cross_head, 0)
     r.CA[...] = heads.values(r.CPD[0:HR], r.KVR[...])
     trs2 = trs_send(1, nt(r.CA[...], r.PWO[2]))
+    w_relay(1)
     w_ready(3)
 
     def prep_up(i, _):
@@ -697,7 +735,6 @@
         return 0
 
     lax.fori_loop(0, NG, prep_up, 0)
-    w_relay(4, (1,))
 
     HT = 256 if hid % 256 == 0 else hid
     NHT = hid // HT
@@ -726,10 +763,9 @@
     r.RSL[...] = rstd
     r.XT[0] = xh.astype(BF)
     tag3 = tag(r.XT)
-    w_relay(4, (2,))
     up_slot(1)
     up_slot(2)
-    w_relay(4, (3,))
+    w_relay(1)
     up_slot(3)
     wait_all(tag3)
 
@@ -739,6 +775,16 @@
         return 0
 
     lax.fori_loop(0, NHT, up_text, 0)
+
+    def gd_step(i, _):
+        lo = pl.multiple_of(i * GT, GT)
+        cols = pl.ds(lo, GT)
+        full = tn(img(r.DY, cols), r.ACT[...].reshape(IP, hid)) + tn(txt(r.DYT, cols), r.ACTT[...])
+        r.GDN[cols] = full.astype(BF)
+        return 0
+
+    lax.fori_loop(0, NG, gd_step, 0)
+    g_start(4)
     w_ready(4)
 
     def back_text(t, _):
@@ -749,7 +795,6 @@
 
     lax.fori_loop(0, NHT, back_text, 0)
     trs4 = trs_send(3, nt(r.GUT[...], r.W[3]))
-    trs3 = trs_send(2, nt(r.ACTT[...], r.W[4]))
 
     def back_slot(i, _):
         s, t = i // NHT, i % NHT
@@ -763,22 +808,19 @@
     r.GTX[...] = gtl
     r.DC[0] = (gtl * r.valid_t[...]).astype(BF)
     tag4 = tag(r.DC)
-
-    def down_out(s, cols):
-        return nt(r.ACT[s], r.W[4, cols])
-
-    st2 = rs_far(1, down_out)
-    rs_near(st2, down_out)
-
-    def gd_step(i, _):
+    trs3 = trs_send(2, nt(r.ACTT[...], r.W[4]))
+
+    def gu_step(i, _):
         lo = pl.multiple_of(i * GT, GT)
         cols = pl.ds(lo, GT)
-        full = tn(img(r.DY, cols), r.ACT[...].reshape(IP, hid)) + tn(txt(r.DYT, cols), r.ACTT[...])
-        r.W[4, cols] = full.astype(BF)
-        return 0
-
-    lax.fori_loop(0, NG, gd_step, 0)
-    g_start(4)
+        full = tn(img(r.X2, cols), r.GU[...].reshape(IP, hid)) + tn(txt(r.XT, cols), r.GUT[...])
+        add_gain(4, lo, full * r.W[3, cols].astype(F32))
+        r.GUP[cols] = (full * gain_col(4, lo)).astype(BF)
+        return 0
+
+    lax.fori_loop(0, NG, gu_step, 0)
+    g_start(3)
+    g_mid(2)
 
     wait_all(tag4)
     da = nn(r.DC[...].reshape(TP, D), r.PWO[2]).astype(BF)
@@ -804,42 +846,12 @@
     def mid_partial(s, cols):
         return nt(r.GU[s], r.W[3, cols]) + nt(r.DKV[s * IR : (s + 1) * IR], r.W[2, cols, KV])
 
+    g_mid(1)
     st3 = rs_far(0, mid_partial)
     rs_over(st3)
     rs_near(st3, mid_partial)
 
-    def gu_step(i, _):
-        lo = pl.multiple_of(i * GT, GT)
-        cols = pl.ds(lo, GT)
-        full = tn(img(r.X2, cols), r.GU[...].reshape(IP, hid)) + tn(txt(r.XT, cols), r.GUT[...])
-        add_gain(4, lo, full * r.W[3, cols].astype(F32))
-        r.W[3, cols] = (full * gain_col(4, lo)).astype(BF)
-        return 0
-
-    lax.fori_loop(0, NG, gu_step, 0)
-    g_start(3)
-    g_mid(4)
-
-    ag3 = []
-
-    def grad_chunk(i):
-        lo, n = CH[i]
-        rows = pl.ds(lo, n)
-        gm = r.GM[rows] + ln_bwd(rs_sum(st3, i), r.XH2[rows], r.RS2[rows])
-        r.GM[rows] = gm
-        r.DY[0, rows] = (gm * r.valid_i[rows]).astype(BF)
-        ag3.append(ag_send(r.DY, lo, n))
-
-    for i in range(len(CH) - 1):
-        grad_chunk(i)
-    gtm = r.GTX[...] + ln_bwd(trs_sum(4, trs5), r.XHQ[...], r.RSQ[...])
-    r.GTX[...] = gtm
-    r.DWT[0] = (gtm * r.valid_t[...]).astype(BF)
-    tag5 = tag(r.DWT)
-    grad_chunk(len(CH) - 1)
-    rs_over(st2)
-    r.text_out[0] = r.TMID[...] + r.valid_t[...] * trs_sum(2, trs3)
-
+    g_mid(2)
     grads_attn(
         2,
         SEGS[2],
@@ -850,6 +862,36 @@
         ),
     )
     g_start(2)
+
+    g_mid(1)
+
+    ag3 = []
+
+    def grad_chunk(i):
+        lo, n = CH[i]
+        rows = pl.ds(lo, n)
+        gm = r.GM[rows] + ln_bwd(rs_sum(st3, i), r.XH2[rows], r.RS2[rows])
+        r.GM[rows] = gm
+        r.DY[0, rows] = (gm * r.valid_i[rows]).astype(BF)
+        ag3.append(ag_send(r.DY, lo, n))
+
+    for i in range(len(CH) - 1):
+        grad_chunk(i)
+    gtm = r.GTX[...] + ln_bwd(trs_sum(4, trs5), r.XHQ[...], r.RSQ[...])
+    r.GTX[...] = gtm
+    r.DWT[0] = (gtm * r.valid_t[...]).astype(BF)
+    tag5 = tag(r.DWT)
+    grad_chunk(len(CH) - 1)
+
+    def down_out(s, cols):
+        return nt(r.ACT[s], r.W[4, cols])
+
+    st2 = rs_far(1, down_out)
+    rs_over(st2)
+    rs_near(st2, down_out)
+    g_mid(2)
+    r.text_out[0] = r.TMID[...] + r.valid_t[...] * trs_sum(2, trs3)
+    emit("text_out")
 
     wait_all(tag5)
     da = nn(r.DWT[...].reshape(TP, D), r.PWO[1]).astype(BF)
@@ -866,6 +908,7 @@
         ),
     )
     g_start(1)
+    g_mid(1)
     rel3 = ag_relay(r.DY, ag3)
     wait_all([a[1] for a in ag3] + rel3)
 
@@ -883,7 +926,7 @@
         return 0
 
     lax.fori_loop(0, COUNT * AREA // WG, perm_d, 0)
-    g_mid(3)
+    g_mid(1)
 
     def win_bwd(w, _):
         at = pl.ds(pl.multiple_of(w * AREA, AREA), AREA)
@@ -897,12 +940,6 @@
     for lo, n in MC:
         r.QR[lo : lo + n] = tn(r.P[:, lo : lo + n], r.QW[...]).astype(BF)
 
-    def win_partial(s, cols):
-        return nt(r.QR[s * IR : (s + 1) * IR], r.W[0, cols, KVQ])
-
-    st4 = rs_far(0, win_partial)
-    rs_over(st4)
-    rs_near(st4, win_partial)
     grads_attn(
         0,
         SEGS[0],
@@ -911,53 +948,64 @@
             lambda cols: tn(img(r.DY, cols), r.AR[...]),
         ),
     )
+    r.GB[0] = jnp.swapaxes(r.GA[...], 0, 1)[0:8]
+    if fused:
+        gc = push(r.GB.at[0], r.GR.at[0], xpeer)
     g_start(0)
+
+    def win_partial(s, cols):
+        return nt(r.QR[s * IR : (s + 1) * IR], r.W[0, cols, KVQ])
+
+    st4 = rs_far(0, win_partial)
+    if fused:
+        gc.wait_recv()
+        r.GB[1] = r.GB[0] + r.GR[0]
+    else:
+        r.GB[1] = r.GB[0]
+    gc = push(r.GB.at[1], r.GR.at[1], yp)
+    rs_over(st4)
+    rs_near(st4, win_partial)
+    gc.wait_recv()
+    part = r.GB[1] + r.GR[1]
+    if fused:
+        r.GZ[z] = part
+        gcs = [
+            push(r.GZ.at[z], r.GZ.at[z], zpeer(d), r.GZ.at[zback(d)]) for d in range(1, nz)
+        ]
+    g_mid(2)
+
+    r.text_grad[0] = r.GTX[...] + ln_bwd(trs_sum(5, trs6), r.XHA[...], r.RSA[...])
+    emit("text_grad")
+    if fused:
+        wait_all(gcs)
+        part = r.GZ[0]
+        for d in range(1, nz):
+            part = part + r.GZ[d]
+    r.GB[2] = part
+    gc = push(r.GB.at[2], r.GR.at[2], core)
     g_mid(1)
-
-    r.GB[0] = jnp.swapaxes(r.GA[...], 0, 1)[0:8]
-    gc = push(r.GB.at[0], r.GR.at[0], core)
-    r.text_grad[0] = r.GTX[...] + ln_bwd(trs_sum(5, trs6), r.XHA[...], r.RSA[...])
-    gc.wait_recv()
-    r.GB[1] = r.GB[0] + r.GR[0]
-    gc = push(r.GB.at[1], r.GR.at[1], yp)
     for i in range(len(CH)):
         lo, n = CH[i]
         rows = pl.ds(lo, n)
         r.MID[rows] = r.MID[rows] + r.valid_i[rows] * rs_sum(st2, i)
     out_i = rows_out(0, r.MID, r.image_out)
+    gc.wait_recv()
+    put_gains(r.GB[2] + r.GR[2])
     g_fin(4)
-    gc.wait_recv()
-    if fused:
-        r.GB[2] = r.GB[1] + r.GR[1]
-        gc = push(r.GB.at[2], r.GR.at[2], xpeer)
-        g_fin(3)
-        g_mid(0)
-        gc.wait_recv()
-        r.GZ[z] = r.GB[2] + r.GR[2]
-        gcs = [
-            push(r.GZ.at[z], r.GZ.at[z], zpeer(d), r.GZ.at[zback(d)]) for d in range(1, nz)
-        ]
+    g_fin(3)
+    g_fin(2)
+    g_fin(1)
     for i, (lo, n) in enumerate(CH):
         rows = pl.ds(lo, n)
         r.GM[rows] = r.GM[rows] + ln_bwd(rs_sum(st4, i), r.XH1[rows], r.RS1[rows])
     out_g = rows_out(1, r.GM, r.image_grad)
-    g_fin(2)
-    g_fin(1)
-    if fused:
-        wait_all(gcs)
-        tot = r.GZ[0]
-        for d in range(1, nz):
-            tot = tot + r.GZ[d]
-        put_gains(tot)
-    else:
-        put_gains(r.GB[1] + r.GR[1])
     g_fin(0)
     if not fused:
         for g in range(5):
-            cp = pltpu.make_async_copy(r.W.at[g], r.G_out.at[g], r.lsem.at[g])
+            cp = pltpu.make_async_copy(g_of(g), r.G_out.at[g], r.lsem.at[g])
             cp.start()
             cp.wait()
-    for cp in out_i + out_g:
+    for cp in out_i + out_g + results:
         cp.wait()
     for cp in pending:
         cp.wait_send()
@@ -971,27 +1019,22 @@
     IP, TP = 4 * IR, 4 * TR
     NH = wd // HD
     ROWS = COUNT * AREA
-    vm = pl.BlockSpec(memory_space=pltpu.VMEM)
     hbm = pl.BlockSpec(memory_space=pl.ANY)
-    scalars = ("page_dims", "shifts", "text_length")
-    in_names = list(inputs)
-    smem = pl.BlockSpec(memory_space=pltpu.SMEM)
-    in_specs = [
-        hbm if n in ("wfull", "image", "icot") else smem if n in scalars else vm for n in in_names
-    ]
-    outs = [
-        ("image_out", (cfg.image_shard, 1, D), F32, hbm),
-        ("text_out", (1, TR, D), F32, vm),
-        ("image_grad", (cfg.image_shard, 1, D), F32, hbm),
-        ("text_grad", (1, TR, D), F32, vm),
-    ]
+    large_in = ("wfull", "image", "icot")
+    cfg.small_in = [n for n in inputs if n not in large_in]
+    in_names = [("h_" + n if n in cfg.small_in else n) for n in inputs]
+    small_out = [("text_out", (1, TR, D)), ("text_grad", (1, TR, D))]
     if fused:
         for n in ("window", "text", "cross"):
-            outs += [("g_" + n, (3, sr, wd), F32, vm), ("g_" + n + "_out", (wd, sr), F32, vm)]
-        outs += [("g_up", (sr, hid), F32, vm), ("g_down", (sr, hid), F32, vm)]
-    else:
-        outs += [("G_out", (5, D, D), BF, hbm)]
-    outs += [("gg_" + n, (D,), F32, vm) for n in ("window", "text", "cross", "memory", "mlp")]
+            small_out += [("g_" + n, (3, sr, wd)), ("g_" + n + "_out", (wd, sr))]
+        small_out += [("g_up", (sr, hid)), ("g_down", (sr, hid))]
+    small_out += [("gg_" + n, (D,)) for n in ("window", "text", "cross", "memory", "mlp")]
+    cfg.small_out = [n for n, _ in small_out]
+    outs = [("o_" + n, shape, F32) for n, shape in small_out]
+    outs.insert(0, ("image_out", (cfg.image_shard, 1, D), F32))
+    outs.insert(2, ("image_grad", (cfg.image_shard, 1, D), F32))
+    if not fused:
+        outs.insert(4, ("G_out", (5, D, D), BF))
     V = pltpu.VMEM
     scratch = {
         "W": V((5, D, D), BF),
@@ -1018,6 +1061,9 @@
         "RSA": V((TR, 1), F32),
         "RSQ": V((TR, 1), F32),
         "RSL": V((TR, 1), F32),
+        "GWN": V((D, D), BF),
+        "GUP": V((D, hid), BF),
+        "GDN": V((D, hid), BF),
         "PWO": V((3, D, wd), BF),
         "P": V((ROWS, IP), BF),
         "QR": V((IP, 3 * wd), BF),
@@ -1064,17 +1110,25 @@
             "ZR": V((5, max(nz - 1, 1), sr, D), BF),
             "GZ": V((nz, 8, D), F32),
         }
+    scalars = ("page_dims", "shifts", "text_length")
+    for n in cfg.small_in:
+        space = pltpu.SMEM if n in scalars else V
+        scratch[n] = space(inputs[n].shape, inputs[n].dtype)
+    for n, shape in small_out:
+        scratch[n] = V(shape, F32)
+    scratch["isem"] = pltpu.SemaphoreType.DMA((len(cfg.small_in),))
+    scratch["osem"] = pltpu.SemaphoreType.DMA((len(small_out),))
     cfg.names = in_names + [o[0] for o in outs] + list(scratch)
     return pl.pallas_call(
         functools.partial(kernel, cfg),
         out_shape=[jax.ShapeDtypeStruct(o[1], o[2]) for o in outs],
-        in_specs=in_specs,
-        out_specs=[o[3] for o in outs],
+        in_specs=[hbm] * len(in_names),
+        out_specs=[hbm] * len(outs),
         scratch_shapes=list(scratch.values()),
         compiler_params=pltpu.CompilerParams(
             collective_id=0, has_side_effects=True, vmem_limit_bytes=int(63.25 * 1024 * 1024)
         ),
-    )(*[inputs[n] for n in in_names])
+    )(*inputs.values())
 
 
 def body(

time: 212 us -> 189 us (0.89)
  Pallas kernels: 208 us -> 187 us
    pallas_call x1, Pallas kernels: 205 us -> 183 us  [run_kernel(): pl.pallas_call(functools.partial(kernel, cfg), out_shape=[jax.ShapeDtypeS...]
where the time goes in v2:
time: 189 us; the launch traced here: 188 us
  Pallas kernels  187 us (99%)
    pallas_call x1, Pallas kernels, run_kernel(): pl.pallas_call(functools.partial(kernel, cfg), out_shape=[jax.ShapeDtypeS...  183 us

profile of v2, /device:TPU:9, one launch (start us, length us, event | category | flops | bytes accessed | tf_op | source)
XLA Modules:
  0.0 188.2 jit_solution(7577959142584708496)
XLA Ops:
  1.3 183.3 %shard_map.323 = (f32[324,1,768]{2,1,0:T(1,128)}, f32[1,32,768]{2,1,0:T(8,128)}, f32[324,1,768]{2,1,0:T(1,128)}, f32[1,32,768]{2,1,0:T(8,128)}, f32[3,96,192]{2,...) custom-call(f32[324,1,768]{2,1,0:T(1,128)} %bitcast.8, ...), custom_call_target="tpu_custom_call" | custom-call | tf_op jit(solution)/shard_map/pallas_call | solution.py:1122
  184.6 3.5 %shard_map.324 = (f32[324,1,768]{2,1,0:T(1,128)}, f32[1,32,768]{2,1,0:T(8,128)}, f32[324,1,768]{2,1,0:T(1,128)}, f32[1,32,768]{2,1,0:T(8,128)}, f32[3,96,192]{2,...) custom-call(f32[324,1,768]{2,1,0:T(1,128)} %get-tuple-element.51.ref, ...), custom_call_target="tpu_custom_call" | custom-call | tf_op jit(solution)/shard_map/pallas_call | solution.py:1229

commit v3 on v2

--- a/solution.py
+++ b/solution.py
@@ -109,7 +109,7 @@
         return dkv, dq
 
 
-NSEM = 192
+NSEM = 208
 UNROLL = 3
 
 
@@ -226,41 +226,85 @@
     def rows_of(seq_index):
         return pl.ds(pl.multiple_of(seq_index * sr, sr), sr)
 
-    wz, wx = {}, {}
+    wx, wown, wthird, relays = {}, {}, {}, []
+    inner = (z == 1) | (z == 2)
+    side = z // 2
+    partner = {"seq": (z + 1 - 2 * (z % 2)) * 2 + x}
+    across = {"seq": (2 - side) * 2 + x}
+    came_from = (None, z + 1 - 2 * (z % 2), 2 - side, 3 - 3 * side)
+
+    def half_of(seq_index, h):
+        return pl.ds(pl.multiple_of(seq_index * sr + h * (sr // 2), sr // 2), sr // 2)
+
+    def w_at(g, rows):
+        return r.W.at[g, rows]
 
     def w_send_x(g):
         if fused:
-            own = r.W.at[g, rows_of(sq)]
-            wx[g] = [push(own, own, xpeer, r.W.at[g, rows_of(z * 2 + (1 - x))])]
+            own = w_at(g, rows_of(sq))
+            wx[g] = [push(own, own, xpeer, w_at(g, rows_of(z * 2 + (1 - x))))]
 
     def w_send_z(g):
-        if fused:
-            own = r.W.at[g, rows_of(sq)]
-            wz[g] = [
-                push(own, own, zpeer(d), r.W.at[g, rows_of(zback(d) * 2 + x)])
-                for d in range(1, nz)
-            ]
-
-    relays = [(g, d) for g in range(5) for d in range(1, nz)]
+        if not fused:
+            return
+        own = w_at(g, rows_of(sq))
+        k = counter[0]
+        counter[0] += 3
+
+        def copy(src, dev, send, recv):
+            return pltpu.make_async_remote_copy(
+                src_ref=src, dst_ref=src, send_sem=r.ssem.at[send], recv_sem=r.rsem.at[recv],
+                device_id=dev, device_id_type=MESH,
+            )
+
+        wown[g] = [copy(own, partner, k, k), copy(own, across, k + 1, k + jnp.where(inner, 1, 2))]
+        for cp in wown[g]:
+            cp.start()
+        pending.extend(wown[g])
+        k2 = counter[0]
+        counter[0] += 2
+        wthird[g] = [None] + [
+            copy(w_at(g, rows_of(came_from[i] * 2 + x)), partner, (k, k2, k2 + 1)[i - 1], k + i - 1)
+            for i in (1, 2, 3)
+        ]
+        relays.extend((g, e) for e in range(4))
 
     def w_relay(n):
         for _ in range(n if fused else 0):
             if not relays:
                 return
-            g, d = relays.pop(0)
-            wz[g][d - 1].wait_recv()
-            at = rows_of(zback(d) * 2 + x)
-            wx[g].append(
-                push(r.W.at[g, at], r.W.at[g, at], xpeer, r.W.at[g, rows_of(zback(d) * 2 + (1 - x))])
-            )
+            g, e = relays.pop(0)
+            if e == 0:
+                wx[g][0].wait_recv()
+                mine, theirs = half_of(z * 2 + (1 - x), 0), half_of(came_from[1] * 2 + (1 - x), 0)
+                wx[g].append(push(w_at(g, mine), w_at(g, mine), partner, w_at(g, theirs)))
+                continue
+            cp = wthird[g][e]
+            cp.wait_recv()
+            here, there = came_from[e] * 2 + x, came_from[e] * 2 + (1 - x)
+            if e == 1:
+                here, there = half_of(here, 1), half_of(there, 1)
+            else:
+                here, there = rows_of(here), rows_of(there)
+                pl.when(inner)(cp.start)
+            wx[g].append(push(w_at(g, here), w_at(g, here), xpeer, w_at(g, there)))
+            if e == 3 and g == 0:
+                for later in range(1, 5):
+                    w_send_z(later)
+                    w_send_x(later)
 
     def w_ready(g):
         if not fused:
             return
         while relays and relays[0][0] <= g:
             w_relay(1)
-        wait_all(wx[g])
-        sent(wz[g] + wx[g])
+        wait_all(wx[g][1:])
+        sent(wown[g] + wx[g])
+
+        @pl.when(inner)
+        def _():
+            for cp in wthird[g][2:]:
+                cp.wait_send()
 
     def w_pack(g):
         if g < 3:
@@ -370,6 +414,23 @@
         for s in range(1, 4):
             r.TS[i, s - 1] = part[s * TR : (s + 1) * TR].astype(BF)
         return [push(r.TS.at[i, s], r.TR.at[i, s], peers[s]) for s in range(3)]
+
+    def trs_far(i, part):
+        r.OT[i] = part[0:TR]
+        for s in range(1, 4):
+            r.TS[i, s - 1] = part[s * TR : (s + 1) * TR].astype(BF)
+        return [i, push(r.TS.at[i, 2], r.TR.at[i, 2], core), push(r.TS.at[i, 0], r.TR.at[i, 0], core)]
+
+    def trs_over(st):
+        i, far, _ = st
+        far.wait_recv()
+        r.TS[i, 1] = (r.TS[i, 1].astype(F32) + r.TR[i, 2].astype(F32)).astype(BF)
+        st.append(push(r.TS.at[i, 1], r.TR.at[i, 1], yp))
+
+    def trs_near_sum(st):
+        i = st[0]
+        wait_all(st[2:])
+        return r.OT[i] + r.TR[i, 0].astype(F32) + r.TR[i, 1].astype(F32)
 
     def trs_sum(i, cps):
         wait_all(cps)
@@ -555,8 +616,6 @@
         need("w_text", "w_text_out", "w_cross", "w_cross_out")
         w_pack(1)
         w_pack(2)
-    w_send_z(1)
-    w_send_z(2)
     need("text")
     xh, rstd = ln_fwd(r.text[...])
     r.XHA[...] = xh
@@ -567,10 +626,7 @@
         need("w_up", "w_down")
         w_pack(3)
         w_pack(4)
-    w_send_z(3)
-    w_send_z(4)
-    w_relay(1)
-    w_send_x(1)
+    w_relay(2)
     need("tcot", *(n for n in cfg.small_in if n.startswith("gain")))
     prep_valid()
     prep_gains()
@@ -593,7 +649,6 @@
     NP = COUNT * AREA // PR
     lax.fori_loop(0, NP // 2, perm_rows, 0)
     w_relay(1)
-    w_send_x(2)
     lax.fori_loop(NP // 2, NP, perm_rows, 0)
     rel1 = ag_relay(r.X1, ag1)
     agdy = [ag_send(r.DY, lo, n) for lo, n in CH]
@@ -617,7 +672,6 @@
 
     lax.fori_loop(0, 2, qkv_slot, 0)
     w_relay(1)
-    w_send_x(3)
     WG = 3 * AREA
 
     def perm_q(i, _):
@@ -626,7 +680,7 @@
         return 0
 
     lax.fori_loop(0, COUNT * AREA // WG, perm_q, 0)
-    w_relay(1)
+    w_relay(2)
 
     def win_fwd(w, _):
         at = pl.ds(pl.multiple_of(w * AREA, AREA), AREA)
@@ -641,8 +695,7 @@
         return 0
 
     lax.fori_loop(0, COUNT, win_fwd, 0, unroll=UNROLL)
-    w_relay(1)
-    w_send_x(4)
+    w_relay(2)
     MC = [(lo, min(384, IP - lo)) for lo in range(0, IP, 384)]
     for lo, n in MC:
         r.AR[lo : lo + n] = tn(r.P[:, lo : lo + n], r.AW[...]).astype(BF)
@@ -652,7 +705,9 @@
 
     st1 = rs_far(0, win_out)
     rs_over(st1)
+    w_relay(1)
     rs_near(st1, win_out)
+    w_relay(1)
 
     w_ready(1)
     prep_attn(1, SEGS[1])
@@ -662,8 +717,9 @@
     o, p = heads.attend(r.TQ[:, K], r.TQ[:, KV], r.TQ[:, Q], ok_t)
     r.TA[...] = o
     r.TPR[...] = p
-    trs1 = trs_send(0, nt(r.TA[...], r.PWO[1]))
+    trs1 = trs_far(0, nt(r.TA[...], r.PWO[1]))
     w_relay(2)
+    trs_over(trs1)
     reldy = ag_relay(r.DY, agdy)
 
     ag2 = []
@@ -682,13 +738,13 @@
     for i in range(len(CH) - 1):
         mid_chunk(i)
     w_relay(1)
-    tmid = r.text[...] + r.valid_t[...] * trs_sum(0, trs1)
+    tmid = r.text[...] + r.valid_t[...] * trs_near_sum(trs1)
     r.TMID[...] = tmid
     xh, rstd = ln_fwd(tmid)
     r.XHQ[...] = xh
     r.RSQ[...] = rstd
     r.X2T[0] = xh.astype(BF)
-    tag2 = tag(r.X2T)
+    tag2 = ag_send(r.X2T, 0, TR)
     mid_chunk(len(CH) - 1)
     wait_all([a[1] for a in agdy] + reldy + tagdy)
     sent([a[1] for a in agdy] + [a[0] for a in agdy] + reldy)
@@ -696,10 +752,13 @@
     w_ready(2)
     prep_attn(2, SEGS[2])
     w_relay(2)
-    rel2 = ag_relay(r.X2, ag2)
-    wait_all(tag2)
+    rel2 = ag_relay(r.X2, ag2[:2])
+    w_relay(1)
+    rel2t = ag_relay(r.X2T, [tag2])
+    rel2 += ag_relay(r.X2, ag2[2:])
+    wait_all([tag2[1]] + rel2t)
     r.CQ[...] = (nn(r.X2T[...].reshape(TP, D), r.W[2, :, Q]) * SCALE).astype(BF)
-    w_relay(1)
+    w_relay(2)
     wait_all([a[1] for a in ag2] + rel2)
 
     def kv_slot(i, _):
@@ -709,7 +768,6 @@
         return 0
 
     lax.fori_loop(0, 2, kv_slot, 0)
-    w_relay(1)
     HR = NH * TP
 
     def head(h, width, at):
@@ -764,8 +822,8 @@
     r.XT[0] = xh.astype(BF)
     tag3 = tag(r.XT)
     up_slot(1)
+    w_relay(1)
     up_slot(2)
-    w_relay(1)
     up_slot(3)
     wait_all(tag3)
 
@@ -838,7 +896,7 @@
 
     lax.fori_loop(0, NH, cross_head_back, 0)
     r.CDQ[...] = (merge_heads(nn(r.CPD[HR : 2 * HR], r.KVR[:, K]), heads.own) * SCALE).astype(BF)
-    trs5 = trs_send(4, nt(r.CDQ[...], r.W[2, :, Q]))
+    trs5 = trs_far(4, nt(r.CDQ[...], r.W[2, :, Q]))
     both = jnp.concatenate([das, heads.place_first(r.CQ[...])], 0)
     for lo, n in MC:
         r.DKV[lo : lo + n] = tn(r.CPD[:, lo : lo + n], both).astype(BF)
@@ -847,6 +905,7 @@
         return nt(r.GU[s], r.W[3, cols]) + nt(r.DKV[s * IR : (s + 1) * IR], r.W[2, cols, KV])
 
     g_mid(1)
+    trs_over(trs5)
     st3 = rs_far(0, mid_partial)
     rs_over(st3)
     rs_near(st3, mid_partial)
@@ -877,10 +936,10 @@
 
     for i in range(len(CH) - 1):
         grad_chunk(i)
-    gtm = r.GTX[...] + ln_bwd(trs_sum(4, trs5), r.XHQ[...], r.RSQ[...])
+    gtm = r.GTX[...] + ln_bwd(trs_near_sum(trs5), r.XHQ[...], r.RSQ[...])
     r.GTX[...] = gtm
     r.DWT[0] = (gtm * r.valid_t[...]).astype(BF)
-    tag5 = tag(r.DWT)
+    tag5 = ag_send(r.DWT, 0, TR)
     grad_chunk(len(CH) - 1)
 
     def down_out(s, cols):
@@ -893,7 +952,8 @@
     r.text_out[0] = r.TMID[...] + r.valid_t[...] * trs_sum(2, trs3)
     emit("text_out")
 
-    wait_all(tag5)
+    rel5 = ag_relay(r.DWT, [tag5])
+    wait_all([tag5[1]] + rel5)
     da = nn(r.DWT[...].reshape(TP, D), r.PWO[1]).astype(BF)
     dkv, dq = heads.attend_back(r.TQ[:, K], r.TQ[:, KV], r.TQ[:, Q], r.TPR[...], da)
     r.DTQ[:, KV] = dkv
@@ -1145,7 +1205,7 @@
     TR = text_in.shape[1]
     IR = -(-shard // 16) * 16
     me = lax.axis_index("tp")
-    fused = n_seq % 2 == 0 and sr % 16 == 0
+    fused = n_seq == 8 and sr % 32 == 0
     cfg = SimpleNamespace(
         D=D, wd=wd, hid=hid, IR=IR, TR=TR, nz=n_seq // 2, sr=sr, fused=fused, image_shard=shard
     )

time: 189 us -> 179 us (0.947)
  Pallas kernels: 187 us -> 178 us
    pallas_call x1, Pallas kernels: 183 us -> 174 us  [run_kernel(): pl.pallas_call(functools.partial(kernel, cfg), out_shape=[jax.ShapeDtypeS...]
where the time goes in v3:
time: 179 us
  Pallas kernels  178 us (99%)
    pallas_call x1, Pallas kernels, run_kernel(): pl.pallas_call(functools.partial(kernel, cfg), out_shape=[jax.ShapeDtypeS...  174 us

profile of v3, /device:TPU:9, one launch (start us, length us, event | category | flops | bytes accessed | tf_op | source)
XLA Modules:
  0.0 179.2 jit_solution(16798645975182317224)
XLA Ops:
  1.3 174.2 %shard_map.323 = (f32[324,1,768]{2,1,0:T(1,128)}, f32[1,32,768]{2,1,0:T(8,128)}, f32[324,1,768]{2,1,0:T(1,128)}, f32[1,32,768]{2,1,0:T(8,128)}, f32[3,96,192]{2,...) custom-call(f32[324,1,768]{2,1,0:T(1,128)} %bitcast.8, ...), custom_call_target="tpu_custom_call" | custom-call | tf_op jit(solution)/shard_map/pallas_call | solution.py:1182
  175.6 3.5 %shard_map.324 = (f32[324,1,768]{2,1,0:T(1,128)}, f32[1,32,768]{2,1,0:T(8,128)}, f32[324,1,768]{2,1,0:T(1,128)}, f32[1,32,768]{2,1,0:T(8,128)}, f32[3,96,192]{2,...) custom-call(f32[324,1,768]{2,1,0:T(1,128)} %get-tuple-element.51.ref, ...), custom_call_target="tpu_custom_call" | custom-call | tf_op jit(solution)/shard_map/pallas_call | solution.py:1289

commit v4 on v3

--- a/solution.py
+++ b/solution.py
@@ -98,14 +98,16 @@
 
     def attend(self, k, kv, q, allowed):
         p = softmax(jnp.where(allowed, nt(stack_heads(q, self.own), k), NEG))
-        return self.values(p, kv), p
+        return merge_heads(nn(p, self.values_of(kv)), self.own).astype(BF), p
+
+    def values_of(self, kv):
+        return kv.astype(F32)[:, self.wd :].astype(BF)
 
     def attend_back(self, k, kv, q, p, da):
-        das = self.place_second(da)
-        ds = score_back(p, nt(das, kv))
+        das = stack_heads(da, self.own)
+        ds = score_back(p, nt(das, self.values_of(kv)))
         dq = (merge_heads(nn(ds, k), self.own) * SCALE).astype(BF)
-        both = jnp.concatenate([self.place_first(q), das], 0)
-        dkv = tn(jnp.concatenate([ds, p], 0), both).astype(BF)
+        dkv = jnp.concatenate([tn(ds, stack_heads(q, self.own)), tn(p, das)], 1).astype(BF)
         return dkv, dq
 
 
@@ -492,7 +494,7 @@
     gx, gzc = {}, {}
 
     def g_of(g):
-        return {0: r.GWN, 3: r.GUP, 4: r.GDN}.get(g, r.W.at[g])
+        return {0: r.CPD.at[pl.ds(0, D), pl.ds(0, D)], 3: r.GUP, 4: r.GDN}.get(g, r.W.at[g])
 
     def g_start(g):
         if not fused:
@@ -780,7 +782,7 @@
         r.CPD[rows] = softmax(jnp.where(r.cvalid[...] > 0.0, nt(qm, r.KVR[:, K]), NEG))
         return 0
 
-    lax.fori_loop(0, NH, cross_head, 0)
+    lax.fori_loop(0, NH, cross_head, 0, unroll=True)
     r.CA[...] = heads.values(r.CPD[0:HR], r.KVR[...])
     trs2 = trs_send(1, nt(r.CA[...], r.PWO[2]))
     w_relay(1)
@@ -894,7 +896,7 @@
         r.CPD[pl.ds(pl.multiple_of(HR + h * TP, TP), TP)] = ds
         return 0
 
-    lax.fori_loop(0, NH, cross_head_back, 0)
+    lax.fori_loop(0, NH, cross_head_back, 0, unroll=True)
     r.CDQ[...] = (merge_heads(nn(r.CPD[HR : 2 * HR], r.KVR[:, K]), heads.own) * SCALE).astype(BF)
     trs5 = trs_far(4, nt(r.CDQ[...], r.W[2, :, Q]))
     both = jnp.concatenate([das, heads.place_first(r.CQ[...])], 0)
@@ -910,7 +912,7 @@
     rs_over(st3)
     rs_near(st3, mid_partial)
 
-    g_mid(2)
+    g_mid(1)
     grads_attn(
         2,
         SEGS[2],
@@ -921,6 +923,12 @@
         ),
     )
     g_start(2)
+    sent([a[0] for a in ag2] + [a[1] for a in ag2] + rel2)
+    for i in range(4):
+        n = min(IR, COUNT * AREA - i * IR)
+        for cols in (slice(t * TILE, (t + 1) * TILE) for t in range(NT_)):
+            rows = nn(r.P[i * IR : i * IR + n], r.X1[:, :, cols].reshape(IP, TILE))
+            r.X2[i, 0:n, cols] = rows.astype(BF)
 
     g_mid(1)
 
@@ -973,7 +981,7 @@
     wait_all([a[1] for a in ag3] + rel3)
 
     def da_slot(i, _):
-        r.DA[pl.ds(pl.multiple_of(i * 2 * IR, 2 * IR), 2 * IR)] = nn(
+        r.KVR[pl.ds(pl.multiple_of(i * 2 * IR, 2 * IR), 2 * IR), K] = nn(
             r.DY[pl.ds(i * 2, 2)].reshape(2 * IR, D), r.PWO[0]
         ).astype(BF)
         return 0
@@ -982,7 +990,7 @@
 
     def perm_d(i, _):
         at = pl.ds(pl.multiple_of(i * WG, WG), WG)
-        r.AW[at] = nn(r.P[at], r.DA[...]).astype(BF)
+        r.AW[at] = nn(r.P[at], r.KVR[:, K]).astype(BF)
         return 0
 
     lax.fori_loop(0, COUNT * AREA // WG, perm_d, 0)
@@ -997,14 +1005,11 @@
 
     lax.fori_loop(0, COUNT, win_bwd, 0, unroll=UNROLL)
     g_mid(2)
-    for lo, n in MC:
-        r.QR[lo : lo + n] = tn(r.P[:, lo : lo + n], r.QW[...]).astype(BF)
-
     grads_attn(
         0,
         SEGS[0],
         (
-            lambda cols: tn(img(r.X1, cols), r.QR[...]),
+            lambda cols: tn(img(r.X2, cols)[: COUNT * AREA], r.QW[...]),
             lambda cols: tn(img(r.DY, cols), r.AR[...]),
         ),
     )
@@ -1012,6 +1017,11 @@
     if fused:
         gc = push(r.GB.at[0], r.GR.at[0], xpeer)
     g_start(0)
+
+    for lo, n in MC:
+        r.QR[lo : lo + n] = tn(r.P[:, lo : lo + n], r.QW[...]).astype(BF)
+
+    g_mid(1)
 
     def win_partial(s, cols):
         return nt(r.QR[s * IR : (s + 1) * IR], r.W[0, cols, KVQ])
@@ -1069,7 +1079,7 @@
         cp.wait()
     for cp in pending:
         cp.wait_send()
-    assert counter[0] <= NSEM
+    assert counter[0] <= NSEM and r.CPD.shape[0] >= D and IP >= D
 
 
 def run_kernel(cfg, inputs):
@@ -1121,7 +1131,6 @@
         "RSA": V((TR, 1), F32),
         "RSQ": V((TR, 1), F32),
         "RSL": V((TR, 1), F32),
-        "GWN": V((D, D), BF),
         "GUP": V((D, hid), BF),
         "GDN": V((D, hid), BF),
         "PWO": V((3, D, wd), BF),
@@ -1130,7 +1139,6 @@
         "QW": V((ROWS, 3 * wd), BF),
         "AW": V((ROWS, wd), BF),
         "AR": V((IP, wd), BF),
-        "DA": V((IP, wd), BF),
         "KVR": V((IP, 2 * wd), BF),
         "DKV": V((IP, 2 * wd), BF),
         "CPD": V((2 * NH * TP, IP), BF),

time: 179 us -> 176 us (0.983)
  Pallas kernels: 178 us -> 174 us
    pallas_call x1, Pallas kernels: 174 us -> 171 us  [run_kernel(): pl.pallas_call(functools.partial(kernel, cfg), out_shape=[jax.ShapeDtypeS...]
where the time goes in v4:
time: 176 us
  Pallas kernels  174 us (99%)
    pallas_call x1, Pallas kernels, run_kernel(): pl.pallas_call(functools.partial(kernel, cfg), out_shape=[jax.ShapeDtypeS...  171 us

profile of v4, /device:TPU:9, one launch (start us, length us, event | category | flops | bytes accessed | tf_op | source)
XLA Modules:
  0.0 175.9 jit_solution(2636329026241680283)
XLA Ops:
  1.3 170.9 %shard_map.323 = (f32[324,1,768]{2,1,0:T(1,128)}, f32[1,32,768]{2,1,0:T(8,128)}, f32[324,1,768]{2,1,0:T(1,128)}, f32[1,32,768]{2,1,0:T(8,128)}, f32[3,96,192]{2,...) custom-call(f32[324,1,768]{2,1,0:T(1,128)} %bitcast.8, ...), custom_call_target="tpu_custom_call" | custom-call | tf_op jit(solution)/shard_map/pallas_call | solution.py:1190
  172.2 3.5 %shard_map.324 = (f32[324,1,768]{2,1,0:T(1,128)}, f32[1,32,768]{2,1,0:T(8,128)}, f32[324,1,768]{2,1,0:T(1,128)}, f32[1,32,768]{2,1,0:T(8,128)}, f32[3,96,192]{2,...) custom-call(f32[324,1,768]{2,1,0:T(1,128)} %get-tuple-element.51.ref, ...), custom_call_target="tpu_custom_call" | custom-call | tf_op jit(solution)/shard_map/pallas_call | solution.py:1297

commit v5 on v4

--- a/solution.py
+++ b/solution.py
@@ -960,6 +960,8 @@
     r.text_out[0] = r.TMID[...] + r.valid_t[...] * trs_sum(2, trs3)
     emit("text_out")
 
+    rel3 = ag_relay(r.DY, ag3[:2])
+
     rel5 = ag_relay(r.DWT, [tag5])
     wait_all([tag5[1]] + rel5)
     da = nn(r.DWT[...].reshape(TP, D), r.PWO[1]).astype(BF)
@@ -977,7 +979,7 @@
     )
     g_start(1)
     g_mid(1)
-    rel3 = ag_relay(r.DY, ag3)
+    rel3 += ag_relay(r.DY, ag3[2:])
     wait_all([a[1] for a in ag3] + rel3)
 
     def da_slot(i, _):
@@ -1018,8 +1020,11 @@
         gc = push(r.GB.at[0], r.GR.at[0], xpeer)
     g_start(0)
 
-    for lo, n in MC:
-        r.QR[lo : lo + n] = tn(r.P[:, lo : lo + n], r.QW[...]).astype(BF)
+    def rows_back(parts):
+        for lo, n in parts:
+            r.QR[lo : lo + n] = tn(r.P[:, lo : lo + n], r.QW[...]).astype(BF)
+
+    rows_back([m for m in MC if m[0] + m[1] > 2 * IR])
 
     g_mid(1)
 
@@ -1034,6 +1039,7 @@
         r.GB[1] = r.GB[0]
     gc = push(r.GB.at[1], r.GR.at[1], yp)
     rs_over(st4)
+    rows_back([m for m in MC if m[0] + m[1] <= 2 * IR])
     rs_near(st4, win_partial)
     gc.wait_recv()
     part = r.GB[1] + r.GR[1]

time: 176 us -> 176 us (level)
  no operation moved by 1% of the time
where the time goes in v5:
time: 176 us; the launch traced here: 175 us
  Pallas kernels  174 us (99%)
    pallas_call x1, Pallas kernels, run_kernel(): pl.pallas_call(functools.partial(kernel, cfg), out_shape=[jax.ShapeDtypeS...  171 us

profile of v5, /device:TPU:9, one launch (start us, length us, event | category | flops | bytes accessed | tf_op | source)
XLA Modules:
  0.0 175.5 jit_solution(4028713294071197851)
XLA Ops:
  1.3 170.5 %shard_map.323 = (f32[324,1,768]{2,1,0:T(1,128)}, f32[1,32,768]{2,1,0:T(8,128)}, f32[324,1,768]{2,1,0:T(1,128)}, f32[1,32,768]{2,1,0:T(8,128)}, f32[3,96,192]{2,...) custom-call(f32[324,1,768]{2,1,0:T(1,128)} %bitcast.8, ...), custom_call_target="tpu_custom_call" | custom-call | tf_op jit(solution)/shard_map/pallas_call | solution.py:1196
  171.8 3.5 %shard_map.324 = (f32[324,1,768]{2,1,0:T(1,128)}, f32[1,32,768]{2,1,0:T(8,128)}, f32[324,1,768]{2,1,0:T(1,128)}, f32[1,32,768]{2,1,0:T(8,128)}, f32[3,96,192]{2,...) custom-call(f32[324,1,768]{2,1,0:T(1,128)} %get-tuple-element.51.ref, ...), custom_call_target="tpu_custom_call" | custom-call | tf_op jit(solution)/shard_map/pallas_call | solution.py:1303

commit v6 on v5

--- a/solution.py
+++ b/solution.py
@@ -111,7 +111,7 @@
         return dkv, dq
 
 
-NSEM = 208
+NSEM = 192
 UNROLL = 3
 
 
@@ -199,9 +199,13 @@
     counter = [0]
     pending = []
 
-    def push(src, dst, dev, land=None):
-        k = counter[0]
-        counter[0] += 1
+    places = {}
+
+    def push(src, dst, dev, land=None, key=None):
+        k = places.get(key, counter[0])
+        counter[0] += k == counter[0]
+        if key is not None:
+            places[key] = k
         mk = functools.partial(
             pltpu.make_async_remote_copy,
             send_sem=r.ssem.at[k],
@@ -461,7 +465,7 @@
         last_rs[b] = st
         S3, S2, RC3 = (r.RB.at[b, i] for i in range(3))
         rs_fill(partial, 3, S3)
-        st.c3 = [push(S3.at[pl.ds(lo, n)], RC3.at[pl.ds(lo, n)], core) for lo, n in CH]
+        st.c3 = [push(S3.at[pl.ds(lo, n)], RC3.at[pl.ds(lo, n)], core, key=(3, st.b, lo)) for lo, n in CH]
         rs_fill(partial, 2, S2)
         return st
 
@@ -471,13 +475,13 @@
             cp.wait_recv()
             rows = pl.ds(lo, n)
             S2[rows] = (S2[rows].astype(F32) + RC3[rows].astype(F32)).astype(BF)
-            st.cy.append(push(S2.at[rows], RY.at[rows], yp))
+            st.cy.append(push(S2.at[rows], RY.at[rows], yp, key=(2, st.b, lo)))
 
     def rs_near(st, partial):
         S1, RC1 = r.RB.at[st.b, 0], r.RB.at[st.b, 3]
         sent(st.c3)
         rs_fill(partial, 1, S1)
-        st.c1 = [push(S1.at[pl.ds(lo, n)], RC1.at[pl.ds(lo, n)], core) for lo, n in CH]
+        st.c1 = [push(S1.at[pl.ds(lo, n)], RC1.at[pl.ds(lo, n)], core, key=(1, st.b, lo)) for lo, n in CH]
         rs_fill(partial, 0, r.OB.at[st.b])
 
     def rs_sum(st, i):

time: 176 us -> 175 us (level)
  no operation moved by 1% of the time
where the time goes in v6:
time: 175 us
  Pallas kernels  174 us (99%)
    pallas_call x1, Pallas kernels, run_kernel(): pl.pallas_call(functools.partial(kernel, cfg), out_shape=[jax.ShapeDtypeS...  170 us

profile of v6, /device:TPU:9, one launch (start us, length us, event | category | flops | bytes accessed | tf_op | source)
XLA Modules:
  0.0 175.2 jit_solution(9545617143659977057)
XLA Ops:
  1.3 170.2 %shard_map.323 = (f32[324,1,768]{2,1,0:T(1,128)}, f32[1,32,768]{2,1,0:T(8,128)}, f32[324,1,768]{2,1,0:T(1,128)}, f32[1,32,768]{2,1,0:T(8,128)}, f32[3,96,192]{2,...) custom-call(f32[324,1,768]{2,1,0:T(1,128)} %bitcast.8, ...), custom_call_target="tpu_custom_call" | custom-call | tf_op jit(solution)/shard_map/pallas_call | solution.py:1200
  171.6 3.5 %shard_map.324 = (f32[324,1,768]{2,1,0:T(1,128)}, f32[1,32,768]{2,1,0:T(8,128)}, f32[324,1,768]{2,1,0:T(1,128)}, f32[1,32,768]{2,1,0:T(8,128)}, f32[3,96,192]{2,...) custom-call(f32[324,1,768]{2,1,0:T(1,128)} %get-tuple-element.51.ref, ...), custom_call_target="tpu_custom_call" | custom-call | tf_op jit(solution)/shard_map/pallas_call | solution.py:1307
